TPU v7x, 32 devices: a whole 2x2x4 slice. The times are simulated.
32 devices in a mesh: groups: 2 (over y), fsdp: 4 (over z), dp: 4 (over x, core).
Axes of the slice: x: 2, y: 2, z: 4, core: 2. Of those that a mesh axis runs over, the one named last changes fastest.
Arguments:
- output_gradient: bfloat16 [6144, 4096], P(('groups', 'dp'), 'fsdp'), parts along dimension 0, may hold values from -6 to 6
- hidden: bfloat16 [6144, 16384], P(('groups', 'dp'), 'fsdp'), parts along dimension 0, may hold values from -6 to 6
- frozen_down_weight: bfloat16 [16384, 4096], P('fsdp', 'dp'), may hold values from -0.09375 to 0.09375
- adapter_first_factors: bfloat16 [64, 16384, 64], P(('groups', 'dp'), 'fsdp'), parts along dimension 0, may hold values from -0.046875 to 0.046875
- adapter_second_factors: bfloat16 [64, 64, 4096], P(('groups', 'dp'), None, 'fsdp'), parts along dimension 0, may hold values from -0.09375 to 0.09375
- island_live_rows: int32 [24], P(('groups', 'dp')), parts along dimension 0, may hold values from 33 to 256, as said below
- island_adapter_ids: int32 [24], P(('groups', 'dp')), parts along dimension 0, may hold values from 0 to 31
- owner_slot_adapters: int32 [64], P('groups'), parts along dimension 0, may hold values from 0 to 31, each once
Outputs:
- grad_hidden: bfloat16 [6144, 16384], P(('groups', 'dp'), 'fsdp'), parts along dimension 0
- grad_a: float32 [64, 16384, 64], P(('groups', 'dp'), 'fsdp'), parts along dimension 0
- grad_b: float32 [64, 64, 4096], P(('groups', 'dp'), None, 'fsdp'), parts along dimension 0
There are 2 independent parts, one for each index of `groups`. A program takes and returns all parts, laid end to end along the dimension named above; an argument that names none is the same for every part. Nothing has to cross between parts.
Inputs may be any that keep to these rules, and one draw needn't show every extreme that they name: `island_live_rows`: at least one block in every draw has all 256 rows live. `owner_slot_adapters`: slot j belongs to index j // (32 / 4) of dp.
All inputs are finite; a program needn't handle non-finite values.
Results may differ from a plain program's by a relative error of at most 0.0029.
Values may be sent and summed in bfloat16 or wider, within the bound.
No kernel may reach another device: no remote copies, remote signals or barrier semaphores. Data moves between devices by JAX's collectives and lax.ppermute only.
A program may use at most 320 MiB of HBM per device.

v0:
```python
import jax
import jax.numpy as jnp
from jax import lax
from jax.sharding import PartitionSpec as P

adapter_scale = 2.0
factor_gradient = 0.0625


def on_device(
    output_gradient,
    hidden,
    frozen_down_weight,
    adapter_first_factors,
    adapter_second_factors,
    island_live_rows,
    island_adapter_ids,
    owner_slot_adapters,
):
    rows, ff_local = hidden.shape
    d_local = output_gradient.shape[1]
    nblocks = island_live_rows.shape[0]
    height = rows // nblocks
    adapter_local = adapter_first_factors.shape[0]
    adap_total = owner_slot_adapters.shape[0]
    rank_index = adapter_first_factors.shape[2]
    offset = jnp.arange(rows, dtype=jnp.int32) % height
    valid = offset < jnp.repeat(island_live_rows, height)
    kept = jnp.where(valid[:, None], output_gradient, jnp.zeros((), output_gradient.dtype))
    match = island_adapter_ids[:, None] == owner_slot_adapters[None, :]
    slot_ids = jnp.sum(
        jnp.where(match, jnp.arange(adap_total, dtype=jnp.int32)[None, :], 0), axis=1
    )
    first_slot = lax.axis_index("dp") * adapter_local
    every_a, every_b = (
        lax.all_gather(adapter_first_factors, "dp", axis=0, tiled=True),
        lax.all_gather(adapter_second_factors, "dp", axis=0, tiled=True),
    )
    block_a = jnp.take(every_a, slot_ids, axis=0)
    block_b = jnp.take(every_b, slot_ids, axis=0)
    hid_blocks = hidden.reshape(nblocks, height, ff_local)
    grad_blocks = kept.reshape(nblocks, height, d_local)
    low_part = jnp.einsum("bsf,bfr->bsr", hid_blocks, block_a, preferred_element_type=jnp.float32)
    coef_part = jnp.einsum("bsd,brd->bsr", grad_blocks, block_b, preferred_element_type=jnp.float32)
    summed_total = lax.psum(jnp.concatenate([low_part, coef_part], axis=2), "fsdp")
    low_round = summed_total[:, :, :rank_index].astype(jnp.bfloat16)
    coefficient_rounded = (adapter_scale * summed_total[:, :, rank_index:]).astype(jnp.bfloat16)
    whole_kept = lax.all_gather(kept, "fsdp", axis=1, tiled=True)
    base = lax.dot_general(
        whole_kept,
        lax.all_gather(frozen_down_weight, "dp", axis=1, tiled=True),
        (((1,), (1,)), ((), ())),
        preferred_element_type=jnp.float32,
    )
    extra = jnp.einsum(
        "bsr,bfr->bsf", coefficient_rounded, block_a, preferred_element_type=jnp.float32
    ).reshape(rows, ff_local)
    grad_hidden = (base + extra).astype(jnp.bfloat16)
    term_a = factor_gradient * jnp.einsum(
        "bsf,bsr->bfr", hid_blocks, coefficient_rounded, preferred_element_type=jnp.float32
    )
    second_term = (
        factor_gradient
        * adapter_scale
        * jnp.einsum("bsr,bsd->brd", low_round, grad_blocks, preferred_element_type=jnp.float32)
    )
    all_slots = lax.all_gather(slot_ids, "dp", axis=0, tiled=True)
    every_ta, every_tb = (
        lax.all_gather(term_a, "dp", axis=0, tiled=True),
        lax.all_gather(second_term, "dp", axis=0, tiled=True),
    )
    select = (
        all_slots[None, :] == first_slot + jnp.arange(adapter_local, dtype=jnp.int32)[:, None]
    ).astype(jnp.float32)
    grad_a = jnp.einsum("jk,kfr->jfr", select, every_ta, precision=lax.Precision.HIGHEST)
    grad_b = jnp.einsum("jk,krd->jrd", select, every_tb, precision=lax.Precision.HIGHEST)
    return (grad_hidden, grad_a, grad_b)


def solution(mesh):
    placed = (
        P(("groups", "dp"), "fsdp"),
        P(("groups", "dp"), "fsdp"),
        P("fsdp", "dp"),
        P(("groups", "dp"), "fsdp", None),
        P(("groups", "dp"), None, "fsdp"),
        P(("groups", "dp")),
        P(("groups", "dp")),
        P("groups"),
    )
    return jax.shard_map(
        on_device,
        mesh=mesh,
        in_specs=placed,
        out_specs=(
            P(("groups", "dp"), "fsdp"),
            P(("groups", "dp"), "fsdp", None),
            P(("groups", "dp"), None, "fsdp"),
        ),
        check_vma=False,
    )
```

profile of v0, /device:TPU:11, one launch (start us, length us, event | category | flops | bytes accessed | tf_op | source)
XLA Modules:
  0.0 675.5 jit_solution(4332583970360828230)
XLA Ops:
  7.2 0.0 copy-start.3
  7.2 0.0 copy-start.5
  7.2 0.0 copy-start.4
  7.2 0.0 copy-start.1
  7.2 0.0 all-gather.13.cloned.1.call-start
  7.2 0.7 all-gather.13.cloned.1.call-update
  7.9 0.0 all-gather.11.cloned.1.call-start
  8.0 0.7 all-gather.11.cloned.1.call-update
  8.7 0.0 all-reduce.3.cloned.1.call-start
  8.7 0.0 copy-done.3
  8.7 0.1 broadcast_in_dim.53
  8.8 0.0 copy-done.5
  8.8 0.0 copy-done.4
  8.8 0.2 select_reduce_fusion
  9.1 0.0 copy-done.1
  9.1 0.2 broadcast_select_fusion.1
  9.3 0.0 copy-start
  9.3 35.5 %all-gather.13.cloned.1.call-done = bf16[32,64,1024]{2,1,0:T(8,128)(2,1)} async-done(((bf16[8,64,1024]{2,1,0:T(8,128)(2,1)}), bf16[32,64,1024]{2,1,0:T(8,128)(2,1)}) %all-gather.13.cloned.1.call-update) | async-done | bytes 4194320 | tf_op jit(solution)/shard_map/all_gather | solution.py:37
  44.8 2.8 gather_fusion.1
  47.5 0.6 fusion.7
  48.1 104.2 %all-gather.11.cloned.1.call-done = bf16[32,4096,64]{1,2,0:T(8,128)(2,1)} async-done(((bf16[8,4096,64]{1,2,0:T(8,128)(2,1)}), bf16[32,4096,64]{1,2,0:T(8,128)(2,1)}) %all-gather.11.cloned.1.call-update) | async-done | bytes 16777232 | tf_op jit(solution)/shard_map/all_gather | solution.py:36
  152.3 6.4 gather_fusion
  158.7 4.8 convolution_bitcast_fusion
  163.5 0.8 pad_maximum_fusion
  164.3 0.0 all-reduce.3.cloned.1.call-update
  164.3 0.0 all-gather.17.cloned.1.call-start
  164.4 36.0 %all-reduce.3.cloned.1.call-done = f32[3,256,128]{1,2,0:T(8,128)} async-done(((f32[3,256,128]{1,2,0:T(8,128)}), f32[3,256,128]{1,2,0:T(8,128)}) %all-reduce.3.cloned.1.call-update) | async-done | bytes 393232 | tf_op jit(solution)/shard_map/psum | solution.py:45
  200.3 0.0 copy-done
  200.3 2.2 convolution_multiply_fusion.1
  202.5 0.0 all-gather.17.cloned.1.call-update
  202.6 0.0 all-gather.15.cloned.1.call-start
  202.6 5.8 fusion.3
  208.4 0.0 all-gather.15.cloned.1.call-update
  208.4 0.0 all-gather.7.cloned.1.call-start
  208.5 0.5 all-gather.7.cloned.1.call-update
  209.0 0.0 copy-start.6
  209.0 0.0 copy-start.2
  209.0 0.0 all-gather.9.cloned.1.call-start
  209.1 0.7 all-gather.9.cloned.1.call-update
  209.8 0.0 copy-done.6
  209.8 0.6 dynamic-slice
  211.0 0.2 dynamic-update-slice
  211.3 5.3 all-reduce
  216.6 0.0 copy-done.2
  216.6 6.3 fusion.6
  222.9 9.2 %all-gather.17.cloned.1.call-done = f32[12,64,1024]{2,1,0:T(8,128)} async-done(((f32[3,64,1024]{2,1,0:T(8,128)}), f32[12,64,1024]{2,1,0:T(8,128)}) %all-gather.17.cloned.1.call-update) | async-done | bytes 3145744 | tf_op jit(solution)/shard_map/all_gather | solution.py:70
  232.2 5.1 fusion.4
  237.2 2.5 copy.20
  239.8 76.6 %all-gather.15.cloned.1.call-done = f32[12,4096,64]{1,2,0:T(8,128)} async-done(((f32[3,4096,64]{1,2,0:T(8,128)}), f32[12,4096,64]{1,2,0:T(8,128)}) %all-gather.15.cloned.1.call-update) | async-done | bytes 12582928 | tf_op jit(solution)/shard_map/all_gather | solution.py:69
  316.4 18.3 %fusion = f32[8,4096,64]{1,0,2:T(8,128)S(1)} fusion(f32[12,4096,64]{1,2,0:T(8,128)} %all-gather.15.cloned.1.call-done, s32[12]{0:T(128)S(1)} %all-reduce, s32[8]{0:T(128)S(1)} %iota_add_fusion), kind=kOutput, calls=%fused_computation.2 | convolution fusion | flops 301989984 | bytes 20971600 | tf_op jit(solution)/shard_map/jk,kfr->jfr/dot_general | solution.py:75
  334.7 8.3 %copy.19 = f32[8,4096,64]{1,2,0:T(8,128)} copy(f32[8,4096,64]{1,0,2:T(8,128)S(1)} %fusion) | data formatting | bytes 16777216
  342.9 88.1 %all-gather.7.cloned.1.call-done = bf16[768,4096]{1,0:T(8,128)(2,1)} async-done(((bf16[768,1024]{1,0:T(8,128)(2,1)}), bf16[768,4096]{1,0:T(8,128)(2,1)}) %all-gather.7.cloned.1.call-update) | async-done | bytes 6291472 | tf_op jit(solution)/shard_map/all_gather | solution.py:48
  431.0 203.7 %all-gather.9.cloned.1.call-done = bf16[4096,4096]{1,0:T(8,128)(2,1)} async-done(((bf16[4096,1024]{1,0:T(8,128)(2,1)}), bf16[4096,4096]{1,0:T(8,128)(2,1)}) %all-gather.9.cloned.1.call-update) | async-done | bytes 33554448 | tf_op jit(solution)/shard_map/all_gather | solution.py:51
  634.7 34.0 %fusion.2 = bf16[768,4096]{1,0:T(8,128)(2,1)} fusion(f32[3,256,4096]{2,1,0:T(8,128)} %fusion.6, bf16[768,4096]{1,0:T(8,128)(2,1)} %all-gather.7.cloned.1.call-done, bf16[4096,4096]{1,0:T(8,128)(2,1)} %all-gather.9.cloned.1.call-done), kind=kOutput, calls=%fused_computation.5 | convolution fusion | flops 25776095232 | bytes 58720256 | tf_op jit(solution)/shard_map/dot_general | solution.py:49
  (7 shorter events, 0.0 us)
Async XLA Ops:
  7.2 1.6 copy-start.3
  7.2 1.7 copy-start.5
  7.2 1.6 copy-start.4
  7.2 1.9 copy-start.1
  7.2 37.5 %all-gather.13.cloned.1.call-start = ((), (), s32[]{:S(2)}) async-start(), calls=%async_computation.3 | async-start | bytes 5242880 | tf_op jit(solution)/shard_map/all_gather | solution.py:37
  7.9 144.3 %all-gather.11.cloned.1.call-start = ((), (), s32[]{:S(2)}) async-start(), calls=%async_computation.2 | async-start | bytes 20971520 | tf_op jit(solution)/shard_map/all_gather | solution.py:36
  8.7 191.6 %all-reduce.3.cloned.1.call-start = ((), (), s32[]{:S(2)}) async-start(), calls=%async_computation.4 | async-start | bytes 786432 | tf_op jit(solution)/shard_map/psum | solution.py:45
  9.3 191.1 %copy-start = (bf16[768,1024]{1,0:T(8,128)(2,1)}, bf16[768,1024]{1,0:T(8,128)(2,1)S(1)}, u32[]{:S(2)}) copy-start(bf16[768,1024]{1,0:T(8,128)(2,1)S(1)} %broadcast_select_fusion.1) | copy-start | bytes 4718596
  164.3 67.8 %all-gather.17.cloned.1.call-start = ((), (), s32[]{:S(2)}) async-start(), calls=%async_computation.6 | async-start | bytes 3932160 | tf_op jit(solution)/shard_map/all_gather | solution.py:70
  202.6 113.8 %all-gather.15.cloned.1.call-start = ((), (), s32[]{:S(2)}) async-start(), calls=%async_computation.5 | async-start | bytes 15728640 | tf_op jit(solution)/shard_map/all_gather | solution.py:69
  208.4 222.6 %all-gather.7.cloned.1.call-start = ((), (), s32[]{:S(2)}) async-start(), calls=%async_computation | async-start | bytes 7864320 | tf_op jit(solution)/shard_map/all_gather | solution.py:48
  209.0 0.8 copy-start.6
  209.0 7.6 %copy-start.2 = (f32[3,256,128]{1,2,0:T(8,128)S(1)}, f32[3,256,128]{1,2,0:T(8,128)}, u32[]{:S(2)}) copy-start(f32[3,256,128]{1,2,0:T(8,128)} %all-reduce.3.cloned.1.call-done) | copy-start | bytes 1179652
  209.0 425.7 %all-gather.9.cloned.1.call-start = ((), (), s32[]{:S(2)}) async-start(), calls=%async_computation.1 | async-start | bytes 41943040 | tf_op jit(solution)/shard_map/all_gather | solution.py:51
Sparse Core Ops, SparseCore 0:
  9.6 35.1 all-gather.12
  46.3 105.9 all-gather.10
  164.5 35.8 all-reduce.2
  202.7 29.4 all-gather.16
  234.2 82.1 all-gather.14
  317.9 113.0 all-gather.6
  432.7 201.9 all-gather.8
where the time goes:
time: 678 us; the launch traced here: 676 us
  waiting for transfers between devices  556 us (82%)
  matrix products  77.1 us (11%)
  local copies, waits for them, and re-layouts  20.9 us (3%)
  between operations  14.9 us (2%)
    all_gather x1, waiting for transfers between devices, on_device(): lax.all_gather(frozen_down_weight, 'dp', axis=1, tiled=True)  204 us
    all_gather x1, waiting for transfers between devices, on_device(): lax.all_gather(adapter_first_factors, 'dp', axis=0, tiled=True)  104 us
    all_gather x1, waiting for transfers between devices, on_device(): whole_kept = lax.all_gather(kept, 'fsdp', axis=1, tiled=True)  88.1 us
    all_gather x1, waiting for transfers between devices, on_device(): lax.all_gather(term_a, 'dp', axis=0, tiled=True)  76.6 us
    psum x1, waiting for transfers between devices, on_device(): lax.psum(jnp.concatenate([low_part, coef_part], axis=2), 'fsdp')  36 us
    all_gather x1, waiting for transfers between devices, on_device(): lax.all_gather(adapter_second_factors, 'dp', axis=0, tiled=True)  35.5 us
    dot_general x1, matrix products, on_device(): lax.dot_general(whole_kept, lax.all_gather(frozen_down_weight, 'dp', axis...  34 us
    dot_general x1, matrix products, on_device(): jnp.einsum('jk,kfr->jfr', select, every_ta, precision=lax.Precision.HIGHEST)  18.3 us
  transfers between devices with their start and end apart: 7, of which 7 were waited for; matrix products, arithmetic and copies ran while one was open for 8% of the time, Pallas kernels for 0%

commit v1 on v0

v1 whole, which is shorter than its diff:
```python
import functools

import jax
import jax.numpy as jnp
from jax import lax
from jax.experimental import pallas as pl
from jax.experimental.pallas import tpu as pltpu
from jax.sharding import PartitionSpec as P

adapter_scale = 2.0
factor_gradient = 0.0625
vmem_bytes = 50 * 1024 * 1024
bf16, f32, i32 = jnp.bfloat16, jnp.float32, jnp.int32


def params(cost):
    return dict(
        compiler_params=pltpu.CompilerParams(vmem_limit_bytes=vmem_bytes),
        cost_estimate=pl.CostEstimate(flops=cost[0], bytes_accessed=cost[1], transcendentals=0),
    )


def pick_kernel(pieces, index_ref, source_ref, *refs):
    a_refs, b_refs, out_ref = refs[:pieces], refs[pieces : 2 * pieces], refs[-1]
    source = source_ref[pl.program_id(0)]
    a, b = a_refs[0][0], b_refs[0][0]
    for r in range(1, pieces):
        a = jnp.where(source == r, a_refs[r][0], a)
        b = jnp.where(source == r, b_refs[r][0], b)
    ff = a.shape[1]
    out_ref[0, :, :ff] = a
    out_ref[0, :, ff:] = b


def factor_specs(pieces, count, rank, width):
    return [
        pl.BlockSpec(
            (1, rank, width), lambda i, index, source, r=r: (index[r * count + i], 0, 0)
        )
        for r in range(pieces)
    ]


def pick(index, source, a_pieces, b_pieces):
    count, pieces = source.shape[0], len(a_pieces)
    _, rank, ff = a_pieces[0].shape
    d = b_pieces[0].shape[2]
    return pl.pallas_call(
        functools.partial(pick_kernel, pieces),
        grid_spec=pltpu.PrefetchScalarGridSpec(
            num_scalar_prefetch=2,
            grid=(count,),
            in_specs=factor_specs(pieces, count, rank, ff) + factor_specs(pieces, count, rank, d),
            out_specs=pl.BlockSpec((1, rank, ff + d), lambda i, index, source: (i, 0, 0)),
        ),
        out_shape=jax.ShapeDtypeStruct((count, rank, ff + d), bf16),
        **params((0, 2 * (pieces + 1) * count * rank * (ff + d))),
    )(index, source, *a_pieces, *b_pieces)


def project_kernel(pieces, index_ref, source_ref, *refs):
    a_refs, b_refs = refs[:pieces], refs[pieces : 2 * pieces]
    far_ref, hid_ref, grad_ref, part_ref, block_ref = refs[2 * pieces :]
    source = source_ref[pl.program_id(0)]
    ff = hid_ref.shape[1]
    a, b = far_ref[0, :, :ff], far_ref[0, :, ff:]
    for r in range(pieces):
        a = jnp.where(source == r, a_refs[r][0], a)
        b = jnp.where(source == r, b_refs[r][0], b)
    block_ref[0] = a
    over_last = (((1,), (1,)), ((), ()))
    rank = a.shape[0]
    part_ref[0, :, :rank] = lax.dot_general(
        hid_ref[...], a, over_last, preferred_element_type=f32
    )
    part_ref[0, :, rank:] = lax.dot_general(
        grad_ref[...], b, over_last, preferred_element_type=f32
    )


def project(index, source, a_pieces, b_pieces, far, hidden, grad):
    count, pieces = source.shape[0], len(a_pieces)
    _, rank, ff = a_pieces[0].shape
    d = b_pieces[0].shape[2]
    rows = hidden.shape[0]
    height = rows // count
    own = lambda i, index, source: (i, 0)
    own3 = lambda i, index, source: (i, 0, 0)
    return pl.pallas_call(
        functools.partial(project_kernel, pieces),
        grid_spec=pltpu.PrefetchScalarGridSpec(
            num_scalar_prefetch=2,
            grid=(count,),
            in_specs=factor_specs(pieces, count, rank, ff)
            + factor_specs(pieces, count, rank, d)
            + [
                pl.BlockSpec((1, rank, ff + d), own3),
                pl.BlockSpec((height, ff), own),
                pl.BlockSpec((height, d), own),
            ],
            out_specs=[
                pl.BlockSpec((1, height, 2 * rank), own3),
                pl.BlockSpec((1, rank, ff), own3),
            ],
        ),
        out_shape=[
            jax.ShapeDtypeStruct((count, height, 2 * rank), f32),
            jax.ShapeDtypeStruct((count, rank, ff), bf16),
        ],
        **params((2 * rows * rank * (ff + d), 2 * (rows + (pieces + 2) * count * rank) * (ff + d))),
    )(index, source, *a_pieces, *b_pieces, far, hidden, grad)


def terms_kernel(live_ref, here_ref, there_ref, hid_ref, grad_ref, terms_ref, coef_ref):
    ff = hid_ref.shape[1]
    rank = coef_ref.shape[2]
    total = here_ref[0] + there_ref[0]
    valid = lax.broadcasted_iota(i32, total.shape, 0) < live_ref[pl.program_id(0)]
    total = jnp.where(valid, total, 0.0)
    low = total[:, :rank].astype(bf16)
    coef = (adapter_scale * total[:, rank:]).astype(bf16)
    coef_ref[0] = coef
    over_rows = (((0,), (0,)), ((), ()))
    terms_ref[0, :, :ff] = (
        factor_gradient
        * lax.dot_general(coef, hid_ref[...], over_rows, preferred_element_type=f32)
    ).astype(bf16)
    terms_ref[0, :, ff:] = (
        factor_gradient
        * adapter_scale
        * lax.dot_general(low, grad_ref[...], over_rows, preferred_element_type=f32)
    ).astype(bf16)


def block_terms(live, here, there, hidden, grad):
    count, height, both = here.shape
    rank = both // 2
    rows, ff = hidden.shape
    d = grad.shape[1]
    own = lambda i, live: (i, 0)
    own3 = lambda i, live: (i, 0, 0)
    return pl.pallas_call(
        terms_kernel,
        grid_spec=pltpu.PrefetchScalarGridSpec(
            num_scalar_prefetch=1,
            grid=(count,),
            in_specs=[
                pl.BlockSpec((1, height, both), own3),
                pl.BlockSpec((1, height, both), own3),
                pl.BlockSpec((height, ff), own),
                pl.BlockSpec((height, d), own),
            ],
            out_specs=[
                pl.BlockSpec((1, rank, ff + d), own3),
                pl.BlockSpec((1, height, rank), own3),
            ],
        ),
        out_shape=[
            jax.ShapeDtypeStruct((count, rank, ff + d), bf16),
            jax.ShapeDtypeStruct((count, height, rank), bf16),
        ],
        **params((2 * rows * rank * (ff + d), 2 * (rows + count * rank) * (ff + d))),
    )(live, here, there, hidden, grad)


def base_kernel(pieces, count, scalars_ref, kept_ref, *refs):
    w_refs = refs[:pieces]
    coef_ref, block_ref = refs[pieces : pieces + 2]
    out_ref = refs[-1]
    deep = w_refs[0].shape[1]
    height = coef_ref.shape[1]
    total = None
    for r in range(pieces):
        start = pl.multiple_of(scalars_ref[1 + r] * deep, deep)
        part = lax.dot_general(
            kept_ref[:, pl.ds(start, deep)],
            w_refs[r][...],
            (((1,), (1,)), ((), ())),
            preferred_element_type=f32,
        )
        total = part if total is None else total + part
    for b in range(count):
        extra = jnp.dot(coef_ref[b], block_ref[b], preferred_element_type=f32)
        here = total[b * height : (b + 1) * height] + extra
        valid = lax.broadcasted_iota(i32, here.shape, 0) < scalars_ref[1 + pieces + b]
        out_ref[b * height : (b + 1) * height, :] = jnp.where(valid, here, 0.0).astype(bf16)


def base(scalars, kept, whole, chunk, coef, block_a, held, size, tile):
    rows, depth = kept.shape
    count, rank, ff = block_a.shape
    pieces = len(whole) + len(chunk)
    deep = depth // pieces
    height = rows // count
    once2 = lambda i, s: (0, 0)
    placed = lambda i, s: (s[0] + i, 0)
    in_specs = [pl.BlockSpec((rows, depth), once2)]
    operands = [kept]
    for r in range(pieces):
        if r in whole:
            in_specs.append(pl.BlockSpec((tile, deep), placed))
            operands.append(whole[r])
        else:
            in_specs.append(pl.BlockSpec((tile, deep), lambda i, s: (i, 0)))
            operands.append(chunk[r])
    in_specs += [
        pl.BlockSpec((count, height, rank), lambda i, s: (0, 0, 0)),
        pl.BlockSpec((count, rank, tile), lambda i, s: (0, 0, s[0] + i)),
    ]
    operands += [coef, block_a]
    aliases = {}
    if held is not None:
        in_specs.append(pl.BlockSpec(memory_space=pl.ANY))
        operands.append(held)
        aliases = {len(operands): 0}
    return pl.pallas_call(
        functools.partial(base_kernel, pieces, count),
        grid_spec=pltpu.PrefetchScalarGridSpec(
            num_scalar_prefetch=1,
            grid=(size // tile,),
            in_specs=in_specs,
            out_specs=pl.BlockSpec((rows, tile), lambda i, s: (0, s[0] + i)),
        ),
        out_shape=jax.ShapeDtypeStruct((rows, ff), bf16),
        input_output_aliases=aliases,
        **params((2 * rows * depth * size, 2 * (rows * depth + (rows + depth) * size))),
    )(scalars, *operands)


def merge_kernel(pieces, count, tiles, slots_ref, *refs):
    term_refs, (a_ref, b_ref) = refs[:pieces], refs[pieces:]
    step = pl.program_id(0)

    def put(out_ref):
        out_ref[...] = jnp.zeros_like(out_ref)
        for r in range(pieces):
            for k in range(count):
                slot = slots_ref[r * count + k]

                @pl.when((slot >= 0) & (slot < out_ref.shape[0]))
                def _():
                    out_ref[slot] += term_refs[r][k].astype(f32)

    pl.when(step < tiles)(lambda: put(a_ref))
    pl.when(step >= tiles)(lambda: put(b_ref))


def merge(slots, pieces, local, ff, tile):
    count, rank, both = pieces[0].shape
    tiles = ff // tile
    d = both - ff
    return pl.pallas_call(
        functools.partial(merge_kernel, len(pieces), count, tiles),
        grid_spec=pltpu.PrefetchScalarGridSpec(
            num_scalar_prefetch=1,
            grid=(both // tile,),
            in_specs=[pl.BlockSpec((count, rank, tile), lambda i, s: (0, 0, i))] * len(pieces),
            out_specs=[
                pl.BlockSpec((local, rank, tile), lambda i, s: (0, 0, jnp.minimum(i, tiles - 1))),
                pl.BlockSpec((local, rank, tile), lambda i, s: (0, 0, jnp.maximum(i - tiles, 0))),
            ],
        ),
        out_shape=[
            jax.ShapeDtypeStruct((local, rank, ff), f32),
            jax.ShapeDtypeStruct((local, rank, d), f32),
        ],
        **params((0, both * rank * (2 * len(pieces) * count + 4 * local))),
    )(slots, *pieces)


def on_device(
    n_groups,
    n_fsdp,
    n_dp,
    output_gradient,
    hidden,
    frozen_down_weight,
    adapter_first_factors,
    adapter_second_factors,
    island_live_rows,
    island_adapter_ids,
    owner_slot_adapters,
):
    rows, ff = hidden.shape
    d = output_gradient.shape[1]
    count = island_live_rows.shape[0]
    local = adapter_first_factors.shape[0]
    n_slots = owner_slot_adapters.shape[0]
    top = n_dp // 2
    me = lax.axis_index("dp")
    group = lax.axis_index("groups")

    def swap(value, bit, axis="dp", size=n_dp):
        return lax.ppermute(value, axis, [(i, i ^ bit) for i in range(size)])

    def spread(held):
        held = dict(held)
        bit = top // 2
        while bit:
            for r in list(held):
                held[r ^ bit] = swap(held[r], bit)
            bit //= 2
        return held

    match = island_adapter_ids[:, None] == owner_slot_adapters[None, :]
    slots = jnp.sum(jnp.where(match, jnp.arange(n_slots, dtype=i32)[None, :], 0), axis=1)
    far_slots = swap(slots, top)

    kept = lax.all_gather(output_gradient, "fsdp", axis=1, tiled=True)

    first = jnp.swapaxes(adapter_first_factors, 1, 2)
    a_near = spread({0: first})
    b_near = spread({0: adapter_second_factors})
    near = sorted(a_near)
    a_near = [a_near[r] for r in near]
    b_near = [b_near[r] for r in near]

    def places(wanted):
        owner = wanted // local
        index = jnp.concatenate([wanted % local] * len(near))
        return index, jnp.where((owner ^ me) < top, owner ^ me, len(near))

    far = swap(pick(*places(far_slots), a_near, b_near), top)

    share = ff // n_groups
    size = max(min(share, 256), share // 4)
    tile = min(512, size)
    shares = []
    for j in range(share // size):
        shares.append(
            swap(
                lax.dynamic_slice_in_dim(
                    frozen_down_weight, group * share + j * size, size, axis=0
                ),
                top,
            )
        )
    whole = spread({0: frozen_down_weight})

    part, block_a = project(*places(slots), a_near, b_near, far, hidden, output_gradient)
    bit = 1
    total = None
    while bit < n_fsdp:
        total = part if total is None else total + other
        other = swap(total, bit, "fsdp", n_fsdp)
        bit *= 2
    terms, coef = block_terms(island_live_rows, total, other, hidden, output_gradient)
    far_terms = swap(terms, top)

    order = [me ^ r for r in range(n_dp)]
    grad_hidden = None
    for shift in range(n_groups):
        for j, piece in enumerate(shares):
            if shift:
                piece = lax.ppermute(
                    piece, "groups", [(i, (i + shift) % n_groups) for i in range(n_groups)]
                )
            start = lax.rem(group + n_groups - shift, n_groups) * share + j * size
            scalars = jnp.stack([start // tile] + order).astype(i32)
            grad_hidden = base(
                jnp.concatenate([scalars, island_live_rows]),
                kept,
                whole,
                spread({top: piece}),
                coef,
                block_a,
                grad_hidden,
                size,
                tile,
            )

    all_slots = spread({0: slots, top: far_slots})
    all_terms = spread({0: terms, top: far_terms})
    keys = sorted(all_terms)
    relative = jnp.concatenate([all_slots[r] for r in keys]) - me * local
    grad_a, grad_b = merge(relative, [all_terms[r] for r in keys], local, ff, min(d, 512))
    return grad_hidden, jnp.swapaxes(grad_a, 1, 2), grad_b


def solution(mesh):
    placed = (
        P(("groups", "dp"), "fsdp"),
        P(("groups", "dp"), "fsdp"),
        P("fsdp", "dp"),
        P(("groups", "dp"), "fsdp", None),
        P(("groups", "dp"), None, "fsdp"),
        P(("groups", "dp")),
        P(("groups", "dp")),
        P("groups"),
    )
    sizes = [mesh.shape[name] for name in ("groups", "fsdp", "dp")]
    return jax.shard_map(
        functools.partial(on_device, *sizes),
        mesh=mesh,
        in_specs=placed,
        out_specs=(
            P(("groups", "dp"), "fsdp"),
            P(("groups", "dp"), "fsdp", None),
            P(("groups", "dp"), None, "fsdp"),
        ),
        check_vma=False,
    )
```

time: 678 us -> 333 us (0.49)
  waiting for transfers between devices: 556 us -> 174 us
  Pallas kernels: 0 us -> 96.6 us
  matrix products: 77.1 us -> 0 us
  starting transfers between devices: 0.28 us -> 30.9 us
  local copies, waits for them, and re-layouts: 20.9 us -> 13.9 us
    all_gather x6 -> x1, waiting for transfers between devices: 517 us -> 0.01 us  [on_device(): kept = lax.all_gather(output_gradient, 'fsdp', axis=1, tiled=True)]
    ppermute x0 -> x28, waiting for transfers between devices: none -> 173 us  [the longest x24 117 us: swap(): return lax.ppermute(value, axis, [(i, i ^ bit) for i in range(size)])]
    pallas_call x0 -> x12, Pallas kernels: none -> 96.6 us  [the longest x8 69.8 us: base(): pl.pallas_call(functools.partial(base_kernel, pieces, count), grid_spec=p...]
    dot_general x8 -> x0, matrix products: 77.1 us -> none  [the longest x1 34 us: on_device(): lax.dot_general(whole_kept, lax.all_gather(frozen_down_weight, 'dp', axis...]
    psum x1 -> x0, waiting for transfers between devices: 36 us -> none  [on_device(): lax.psum(jnp.concatenate([low_part, coef_part], axis=2), 'fsdp')]
    ppermute x0 -> x28, starting transfers between devices: none -> 30.9 us  [the longest x24 27 us: swap(): return lax.ppermute(value, axis, [(i, i ^ bit) for i in range(size)])]
    gather x2 -> x0, local copies, waits for them, and re-layouts: 9.17 us -> none  [the longest x1 6.41 us: on_device(): block_a = jnp.take(every_a, slot_ids, axis=0)]
  transfers between devices with their start and end apart: 7 -> 29, of which waited for: 7 -> 13; matrix products, arithmetic and copies ran while one was open for 8% -> 1% of each run, Pallas kernels for 0% -> 26%
where the time goes in v1:
time: 333 us; the launch traced here: 330 us
  waiting for transfers between devices  174 us (52%)
  Pallas kernels  96.6 us (29%)
  starting transfers between devices  30.9 us (9%)
  between operations  14.1 us (4%)
  local copies, waits for them, and re-layouts  13.9 us (4%)
    ppermute x24, waiting for transfers between devices, swap(): return lax.ppermute(value, axis, [(i, i ^ bit) for i in range(size)])  117 us
    pallas_call x8, Pallas kernels, base(): pl.pallas_call(functools.partial(base_kernel, pieces, count), grid_spec=p...  69.8 us
    ppermute x4, waiting for transfers between devices, on_device(): lax.ppermute(piece, 'groups', [(i, (i + shift) % n_groups) for i in range...  55.8 us
    ppermute x24, starting transfers between devices, swap(): return lax.ppermute(value, axis, [(i, i ^ bit) for i in range(size)])  27 us
    unnamed x34, local copies, waits for them, and re-layouts  10.6 us
    pallas_call x1, Pallas kernels, merge(): pl.pallas_call(functools.partial(merge_kernel, len(pieces), count, tiles)...  10.4 us
    pallas_call x1, Pallas kernels, project(): pl.pallas_call(functools.partial(project_kernel, pieces), grid_spec=pltpu...  7.86 us
  transfers between devices with their start and end apart: 29, of which 13 were waited for; matrix products, arithmetic and copies ran while one was open for 1% of the time, Pallas kernels for 26%

profile of v1, /device:TPU:11, one launch (start us, length us, event | category | flops | bytes accessed | tf_op | source)
XLA Modules:
  0.0 330.3 jit_solution(8046554679822652144)
XLA Ops:
  7.2 0.7 all-gather.2.cloned.1.call-update
  7.9 0.7 collective-permute-start.4
  8.7 0.4 collective-permute-start.5
  9.2 0.9 select_reduce_fusion
  10.0 0.3 collective-permute-start.6
  10.3 2.1 collective-permute-done.6
  12.6 5.8 %collective-permute-done.5.refs_3_ = bf16[8,64,1024]{2,1,0:T(8,128)(2,1)S(1)} collective-permute-done((bf16[8,64,1024]{2,1,0:T(8,128)(2,1)}, bf16[8,64,1024]{2,1,0:T(8,128)(2,1)S(1)}, u32[]{:S(2)}, u32[]{:S(2)}) %collective-permute-start.5) | collective-permute-done | bytes 1048608 | tf_op jit(solution)/shard_map/ppermute | solution.py:294
  18.4 1.7 copy-done.1
  20.1 2.1 shard_map.103
  22.2 1.6 collective-permute-start.7
  23.8 2.6 constant_dynamic-slice_fusion
  26.5 1.5 collective-permute-start.13
  28.1 38.3 %collective-permute-done.7.refs_4_ = bf16[3,64,5120]{2,1,0:T(8,128)(2,1)} collective-permute-done((bf16[3,64,5120]{2,1,0:T(8,128)(2,1)S(1)}, bf16[3,64,5120]{2,1,0:T(8,128)(2,1)}, u32[]{:S(2)}, u32[]{:S(2)}) %collective-permute-start.7) | collective-permute-done | bytes 1966112 | tf_op jit(solution)/shard_map/ppermute | solution.py:294
  66.4 2.0 collective-permute-start.23
  68.4 1.2 copy-done.2
  69.6 1.2 copy-done.4
  70.9 7.9 %shard_map.104 = (f32[3,256,128]{2,1,0:T(8,128)S(1)}, bf16[3,64,4096]{2,1,0:T(8,128)(2,1)S(1)}) custom-call(s32[6]{0:T(128)S(1)} %pad_add_fusion.index_ref, s32[3]{0:T(128)S(1)} %get-tuple-element.21.source_ref, bf16[8,64,4096]{2,1,0:T(8,128)(2,1)} %bitcast.16, bf16[8,64,4096]{2,1,0:T(8,128)(2,1)} %collective-permute-done.4.refs_1_, ...), custom_call_target="tpu_custom_call" | custom-call | flops 503316480 | bytes 15728640 | tf_op jit(solution)/shard_map/pallas_call | solution.py:89
  78.8 1.1 collective-permute-done.24
  79.9 0.2 collective-permute-start.8
  80.2 8.7 %collective-permute-done.16.refs_2_ = bf16[512,1024]{1,0:T(8,128)(2,1)S(1)} collective-permute-done((bf16[512,1024]{1,0:T(8,128)(2,1)S(1)}, bf16[512,1024]{1,0:T(8,128)(2,1)S(1)}, u32[]{:S(2)}, u32[]{:S(2)}) %collective-permute-start.16) | collective-permute-done | bytes 1048608 | tf_op jit(solution)/shard_map/ppermute | solution.py:294
  88.9 1.8 collective-permute-start.1
  90.7 20.7 %collective-permute-done.13.refs_2_ = bf16[512,1024]{1,0:T(8,128)(2,1)} collective-permute-done((bf16[512,1024]{1,0:T(8,128)(2,1)S(1)}, bf16[512,1024]{1,0:T(8,128)(2,1)}, u32[]{:S(2)}, u32[]{:S(2)}) %collective-permute-start.13) | collective-permute-done | bytes 1048608 | tf_op jit(solution)/shard_map/ppermute | solution.py:294
  111.4 2.0 collective-permute-start.22
  113.4 6.4 %collective-permute-done.8 = f32[3,256,128]{2,1,0:T(8,128)S(1)} collective-permute-done((f32[3,256,128]{2,1,0:T(8,128)S(1)}, f32[3,256,128]{2,1,0:T(8,128)S(1)}, u32[]{:S(2)}, u32[]{:S(2)}) %collective-permute-start.8) | collective-permute-done | bytes 393248 | tf_op jit(solution)/shard_map/ppermute | solution.py:294
  119.7 0.4 collective-permute-start.21
  120.2 13.7 %collective-permute-done.10.refs_2_ = bf16[512,1024]{1,0:T(8,128)(2,1)} collective-permute-done((bf16[512,1024]{1,0:T(8,128)(2,1)S(1)}, bf16[512,1024]{1,0:T(8,128)(2,1)}, u32[]{:S(2)}, u32[]{:S(2)}) %collective-permute-start.10) | collective-permute-done | bytes 1048608 | tf_op jit(solution)/shard_map/ppermute | solution.py:294
  133.9 2.3 collective-permute-start.9
  136.1 20.2 %collective-permute-done.1.refs_2_ = bf16[512,1024]{1,0:T(8,128)(2,1)} collective-permute-done((bf16[512,1024]{1,0:T(8,128)(2,1)S(1)}, bf16[512,1024]{1,0:T(8,128)(2,1)}, u32[]{:S(2)}, u32[]{:S(2)}) %collective-permute-start.1) | collective-permute-done | bytes 1048608 | tf_op jit(solution)/shard_map/ppermute | solution.py:294
  156.3 1.2 collective-permute-start.20
  157.5 6.4 %shard_map.105 = (bf16[3,64,5120]{2,1,0:T(8,128)(2,1)}, bf16[3,256,64]{2,1,0:T(8,128)(2,1)S(1)}) custom-call(s32[3]{0:T(128)S(1)} %copy-done.16, f32[3,256,128]{2,1,0:T(8,128)S(1)} %add.86.here_ref, f32[3,256,128]{2,1,0:T(8,128)S(1)} %collective-permute-done.9.there_ref, bf16[768,4096]{1,0:T(8,128)(2,1)} %hid_ref.1, bf16[768,1024]{1,0:T(8,128)(2,1)S(1)} %copy-done), custom_call_target="tpu_custom_call" | custom-call | flops 503316480 | bytes 9830400 | tf_op jit(solution)/shard_map/pallas_call | solution.py:142
  164.0 1.0 copy-done.8
  164.9 1.5 collective-permute-start.26
  166.4 1.0 copy-done.10
  167.4 1.2 collective-permute-start.17
  168.6 1.0 copy-done.14
  169.6 0.3 collective-permute-start.14
  169.9 1.0 copy-done.12
  170.8 1.2 collective-permute-start.11
  172.0 19.4 %collective-permute-done.17.refs_2_ = bf16[512,1024]{1,0:T(8,128)(2,1)} collective-permute-done((bf16[512,1024]{1,0:T(8,128)(2,1)S(1)}, bf16[512,1024]{1,0:T(8,128)(2,1)}, u32[]{:S(2)}, u32[]{:S(2)}) %collective-permute-start.17) | collective-permute-done | bytes 1048608 | tf_op jit(solution)/shard_map/ppermute | solution.py:355
  191.4 1.2 collective-permute-start.2
  192.6 3.2 collective-permute-start.18
  195.8 0.1 concatenate.42.scalars_ref
  195.9 0.1 concatenate.41.scalars_ref
  196.0 0.1 concatenate.40.scalars_ref
  196.2 0.1 concatenate.38.scalars_ref
  196.3 0.1 concatenate.37.scalars_ref
  196.4 0.1 concatenate.33.scalars_ref
  196.6 1.2 copy-done.7
  197.8 1.2 copy-done.9
  199.1 8.7 %shard_map.106.refs_6_ = bf16[768,4096]{1,0:T(8,128)(2,1)} custom-call(s32[8]{0:T(128)S(1)} %concatenate.42.scalars_ref, bf16[768,4096]{1,0:T(8,128)(2,1)} %all-gather.2.cloned.1.call-done.kept_ref, bf16[4096,1024]{1,0:T(8,128)(2,1)} %refs_0_.15, bf16[4096,1024]{1,0:T(8,128)(2,1)} %collective-permute-done.refs_1_, bf16[512,1024]{1,0:T(8,128)(2,1)S(1)} %copy-done.7, ...), custom_call_target="tpu_custom_call" | custom-call | flops 3221225472 | bytes 11272192 | tf_op jit(solution)/shard_map/pallas_call | solution.py:216
  207.7 6.2 %collective-permute-done.14.refs_2_ = bf16[512,1024]{1,0:T(8,128)(2,1)} collective-permute-done((bf16[512,1024]{1,0:T(8,128)(2,1)}, bf16[512,1024]{1,0:T(8,128)(2,1)}, u32[]{:S(2)}, u32[]{:S(2)}) %collective-permute-start.14) | collective-permute-done | bytes 1048608 | tf_op jit(solution)/shard_map/ppermute | solution.py:355
  213.9 2.9 collective-permute-start.15
  216.8 19.5 %collective-permute-done.11.refs_2_ = bf16[512,1024]{1,0:T(8,128)(2,1)} collective-permute-done((bf16[512,1024]{1,0:T(8,128)(2,1)}, bf16[512,1024]{1,0:T(8,128)(2,1)}, u32[]{:S(2)}, u32[]{:S(2)}) %collective-permute-start.11) | collective-permute-done | bytes 1048608 | tf_op jit(solution)/shard_map/ppermute | solution.py:355
  236.4 2.9 collective-permute-start.25
  239.4 8.7 %shard_map.107.refs_6_ = bf16[768,4096]{1,0:T(8,128)(2,1)} custom-call(s32[8]{0:T(128)S(1)} %concatenate.41.scalars_ref, bf16[768,4096]{1,0:T(8,128)(2,1)} %all-gather.2.cloned.1.call-done.kept_ref, bf16[4096,1024]{1,0:T(8,128)(2,1)} %refs_0_.15, bf16[4096,1024]{1,0:T(8,128)(2,1)} %collective-permute-done.refs_1_, ...), custom_call_target="tpu_custom_call", output_to_operand_aliasing={{}: (8, {})} | custom-call | flops 3221225472 | bytes 11272192 | tf_op jit(solution)/shard_map/pallas_call | solution.py:216
  248.1 10.8 %collective-permute-done.2.refs_2_ = bf16[512,1024]{1,0:T(8,128)(2,1)} collective-permute-done((bf16[512,1024]{1,0:T(8,128)(2,1)}, bf16[512,1024]{1,0:T(8,128)(2,1)}, u32[]{:S(2)}, u32[]{:S(2)}) %collective-permute-start.2) | collective-permute-done | bytes 1048608 | tf_op jit(solution)/shard_map/ppermute | solution.py:355
  258.8 1.7 collective-permute-start.12
  260.5 8.7 %shard_map.108.refs_6_ = bf16[768,4096]{1,0:T(8,128)(2,1)} custom-call(s32[8]{0:T(128)S(1)} %concatenate.40.scalars_ref, bf16[768,4096]{1,0:T(8,128)(2,1)} %all-gather.2.cloned.1.call-done.kept_ref, bf16[4096,1024]{1,0:T(8,128)(2,1)} %refs_0_.15, bf16[4096,1024]{1,0:T(8,128)(2,1)} %collective-permute-done.refs_1_, ...), custom_call_target="tpu_custom_call", output_to_operand_aliasing={{}: (8, {})} | custom-call | flops 3221225472 | bytes 11272192 | tf_op jit(solution)/shard_map/pallas_call | solution.py:216
  269.2 8.7 %shard_map.109.refs_6_ = bf16[768,4096]{1,0:T(8,128)(2,1)} custom-call(s32[8]{0:T(128)S(1)} %concatenate.39.scalars_ref, bf16[768,4096]{1,0:T(8,128)(2,1)} %all-gather.2.cloned.1.call-done.kept_ref, bf16[4096,1024]{1,0:T(8,128)(2,1)} %refs_0_.15, bf16[4096,1024]{1,0:T(8,128)(2,1)} %collective-permute-done.refs_1_, ...), custom_call_target="tpu_custom_call", output_to_operand_aliasing={{}: (8, {})} | custom-call | flops 3221225472 | bytes 11272192 | tf_op jit(solution)/shard_map/pallas_call | solution.py:216
  277.9 9.0 %shard_map.110.refs_6_ = bf16[768,4096]{1,0:T(8,128)(2,1)} custom-call(s32[8]{0:T(128)S(1)} %concatenate.38.scalars_ref, bf16[768,4096]{1,0:T(8,128)(2,1)} %all-gather.2.cloned.1.call-done.kept_ref, bf16[4096,1024]{1,0:T(8,128)(2,1)} %refs_0_.15, bf16[4096,1024]{1,0:T(8,128)(2,1)} %collective-permute-done.refs_1_, ...), custom_call_target="tpu_custom_call", output_to_operand_aliasing={{}: (8, {})} | custom-call | flops 3221225472 | bytes 11272192 | tf_op jit(solution)/shard_map/pallas_call | solution.py:216
  286.9 8.7 %shard_map.111.refs_6_ = bf16[768,4096]{1,0:T(8,128)(2,1)} custom-call(s32[8]{0:T(128)S(1)} %concatenate.37.scalars_ref, bf16[768,4096]{1,0:T(8,128)(2,1)} %all-gather.2.cloned.1.call-done.kept_ref, bf16[4096,1024]{1,0:T(8,128)(2,1)} %refs_0_.15, bf16[4096,1024]{1,0:T(8,128)(2,1)} %collective-permute-done.refs_1_, ...), custom_call_target="tpu_custom_call", output_to_operand_aliasing={{}: (8, {})} | custom-call | flops 3221225472 | bytes 11272192 | tf_op jit(solution)/shard_map/pallas_call | solution.py:216
  295.6 8.7 %shard_map.112.refs_6_ = bf16[768,4096]{1,0:T(8,128)(2,1)} custom-call(s32[8]{0:T(128)S(1)} %concatenate.36.scalars_ref, bf16[768,4096]{1,0:T(8,128)(2,1)} %all-gather.2.cloned.1.call-done.kept_ref, bf16[4096,1024]{1,0:T(8,128)(2,1)} %refs_0_.15, bf16[4096,1024]{1,0:T(8,128)(2,1)} %collective-permute-done.refs_1_, ...), custom_call_target="tpu_custom_call", output_to_operand_aliasing={{}: (8, {})} | custom-call | flops 3221225472 | bytes 11272192 | tf_op jit(solution)/shard_map/pallas_call | solution.py:216
  304.3 8.7 %shard_map.113 = bf16[768,4096]{1,0:T(8,128)(2,1)} custom-call(s32[8]{0:T(128)S(1)} %concatenate.33.scalars_ref, bf16[768,4096]{1,0:T(8,128)(2,1)} %all-gather.2.cloned.1.call-done.kept_ref, bf16[4096,1024]{1,0:T(8,128)(2,1)} %refs_0_.15, bf16[4096,1024]{1,0:T(8,128)(2,1)} %collective-permute-done.refs_1_, ...), custom_call_target="tpu_custom_call", output_to_operand_aliasing={{}: (8, {})} | custom-call | flops 3221225472 | bytes 11272192 | tf_op jit(solution)/shard_map/pallas_call | solution.py:216
  313.0 10.4 %shard_map.114 = (f32[8,64,4096]{2,1,0:T(8,128)}, f32[8,64,1024]{2,1,0:T(8,128)}) custom-call(s32[12]{0:T(128)S(1)} %add_subtract_fusion.slots_ref, bf16[3,64,5120]{2,1,0:T(8,128)(2,1)S(1)} %copy-done.5, bf16[3,64,5120]{2,1,0:T(8,128)(2,1)S(1)} %collective-permute-done.25.refs_1_, bf16[3,64,5120]{2,1,0:T(8,128)(2,1)} %collective-permute-done.26.refs_2_, ...), custom_call_target="tpu_custom_call" | custom-call | bytes 18350080 | tf_op jit(solution)/shard_map/pallas_call | solution.py:252
  (57 shorter events, 1.0 us)
Async XLA Ops:
  7.2 189.4 %all-gather.2.cloned.1.call-start = ((), (), s32[]{:S(2)}) async-start(), calls=%async_computation | async-start | bytes 7864320 | tf_op jit(solution)/shard_map/all_gather | solution.py:309
  7.9 10.5 %collective-permute-start.4 = (bf16[8,64,4096]{2,1,0:T(8,128)(2,1)}, bf16[8,64,4096]{2,1,0:T(8,128)(2,1)}, u32[]{:S(2)}, u32[]{:S(2)}) collective-permute-start(bf16[8,64,4096]{2,1,0:T(8,128)(2,1)} %bitcast.14), channel_id=1, source_target_pairs={{0,1},{1,0},{2,3},{3,2},{4,5},{5,4},{6,7},{7,6},{8,9},{9,8},{10,11... | collective-permute-start | bytes 12582920 | tf_op jit(solution)/shard_map/ppermute | solution.py:294
  8.6 184.0 %collective-permute-start = (bf16[4096,1024]{1,0:T(8,128)(2,1)}, bf16[4096,1024]{1,0:T(8,128)(2,1)}, u32[]{:S(2)}, u32[]{:S(2)}) collective-permute-start(bf16[4096,1024]{1,0:T(8,128)(2,1)} %refs_0_.15), channel_id=1, source_target_pairs={{0,1},{1,0},{2,3},{3,2},{4,5},{5,4},{6,7},{7,6},{8,9},{9,8},{10,11... | collective-permute-start | bytes 25165832 | tf_op jit(solution)/shard_map/ppermute | solution.py:294
  8.7 9.6 %collective-permute-start.5 = (bf16[8,64,1024]{2,1,0:T(8,128)(2,1)}, bf16[8,64,1024]{2,1,0:T(8,128)(2,1)S(1)}, u32[]{:S(2)}, u32[]{:S(2)}) collective-permute-start(bf16[8,64,1024]{2,1,0:T(8,128)(2,1)} %refs_2_.3), channel_id=1, source_target_pairs={{0,1},{1,0},{2,3},{3,2},{4,5},{5,4},{6,7},{7,6},{8,9},{9,8},{10,11... | collective-permute-start | bytes 3145736 | tf_op jit(solution)/shard_map/ppermute | solution.py:294
  10.0 2.5 collective-permute-start.6
  18.3 8.1 %copy-start.3 = (bf16[8,64,1024]{2,1,0:T(8,128)(2,1)}, bf16[8,64,1024]{2,1,0:T(8,128)(2,1)S(1)}, u32[]{:S(2)}) copy-start(bf16[8,64,1024]{2,1,0:T(8,128)(2,1)S(1)} %collective-permute-done.5.refs_3_) | copy-start | bytes 3145732
  18.4 1.7 copy-start.1
  22.2 44.3 %collective-permute-start.7 = (bf16[3,64,5120]{2,1,0:T(8,128)(2,1)S(1)}, bf16[3,64,5120]{2,1,0:T(8,128)(2,1)}, u32[]{:S(2)}, u32[]{:S(2)}) collective-permute-start(bf16[3,64,5120]{2,1,0:T(8,128)(2,1)S(1)} %shard_map.103), channel_id=1, source_target_pairs={{0,2},{1,3},{2,0},{3,1},{4,6},{5,7},{6,4},{7,5},{8,10},{9,11},{10,... | collective-permute-start | bytes 5898248 | tf_op jit(solution)/shard_map/ppermute | solution.py:294
  26.4 62.5 %collective-permute-start.16 = (bf16[512,1024]{1,0:T(8,128)(2,1)S(1)}, bf16[512,1024]{1,0:T(8,128)(2,1)S(1)}, u32[]{:S(2)}, u32[]{:S(2)}) collective-permute-start(bf16[512,1024]{1,0:T(8,128)(2,1)S(1)} %get-tuple-element.15), channel_id=1, source_target_pairs={{0,2},{1,3},{2,0},{3,1},{4,6},{5,7},{6,4},{7,5},{8,10},{9,11},{10,... | collective-permute-start | bytes 3145736 | tf_op jit(solution)/shard_map/ppermute | solution.py:294
  26.5 84.9 %collective-permute-start.13 = (bf16[512,1024]{1,0:T(8,128)(2,1)S(1)}, bf16[512,1024]{1,0:T(8,128)(2,1)}, u32[]{:S(2)}, u32[]{:S(2)}) collective-permute-start(bf16[512,1024]{1,0:T(8,128)(2,1)S(1)} %get-tuple-element.16), channel_id=1, source_target_pairs={{0,2},{1,3},{2,0},{3,1},{4,6},{5,7},{6,4},{7,5},{8,10},{9,11},{10,... | collective-permute-start | bytes 3145736 | tf_op jit(solution)/shard_map/ppermute | solution.py:294
  27.9 105.9 %collective-permute-start.10 = (bf16[512,1024]{1,0:T(8,128)(2,1)S(1)}, bf16[512,1024]{1,0:T(8,128)(2,1)}, u32[]{:S(2)}, u32[]{:S(2)}) collective-permute-start(bf16[512,1024]{1,0:T(8,128)(2,1)S(1)} %get-tuple-element.17), channel_id=1, source_target_pairs={{0,2},{1,3},{2,0},{3,1},{4,6},{5,7},{6,4},{7,5},{8,10},{9,11},{10,... | collective-permute-start | bytes 3145736 | tf_op jit(solution)/shard_map/ppermute | solution.py:294
  66.4 12.3 %collective-permute-start.23 = (s32[3]{0:T(128)S(1)}, s32[3]{0:T(128)S(1)}, u32[]{:S(2)}, u32[]{:S(2)}) collective-permute-start(s32[3]{0:T(128)S(1)} %select_reduce_fusion), channel_id=1, source_target_pairs={{0,1},{1,0},{2,3},{3,2},{4,5},{5,4},{6,7},{7,6},{8,9},{9,8},{10,11... | collective-permute-start | bytes 44 | tf_op jit(solution)/shard_map/ppermute | solution.py:294
  68.4 1.2 copy-start.2
  69.6 1.2 copy-start.4
  70.9 86.7 %copy-start = (bf16[768,1024]{1,0:T(8,128)(2,1)S(1)}, bf16[768,1024]{1,0:T(8,128)(2,1)}, u32[]{:S(2)}) copy-start(bf16[768,1024]{1,0:T(8,128)(2,1)} %grad_ref.1) | copy-start | bytes 4718596
  70.9 86.7 %copy-start.16 = (s32[3]{0:T(128)S(1)}, s32[3]{0:T(128)}, u32[]{:S(2)}) copy-start(s32[3]{0:T(128)} %live_ref.1) | copy-start | bytes 40
  78.8 1.2 collective-permute-start.24
  79.9 39.8 %collective-permute-start.8 = (f32[3,256,128]{2,1,0:T(8,128)S(1)}, f32[3,256,128]{2,1,0:T(8,128)S(1)}, u32[]{:S(2)}, u32[]{:S(2)}) collective-permute-start(f32[3,256,128]{2,1,0:T(8,128)S(1)} %get-tuple-element.9), channel_id=1, source_target_pairs={{0,4},{4,0},{8,12},{12,8},{1,5},{5,1},{9,13},{13,9},{2,6},{6,2},{1... | collective-permute-start | bytes 1179656 | tf_op jit(solution)/shard_map/ppermute | solution.py:294
  88.9 77.5 %copy-start.6 = (bf16[512,1024]{1,0:T(8,128)(2,1)}, bf16[512,1024]{1,0:T(8,128)(2,1)S(1)}, u32[]{:S(2)}) copy-start(bf16[512,1024]{1,0:T(8,128)(2,1)S(1)} %collective-permute-done.16.refs_2_) | copy-start | bytes 3145732
  88.9 67.4 %collective-permute-start.1 = (bf16[512,1024]{1,0:T(8,128)(2,1)S(1)}, bf16[512,1024]{1,0:T(8,128)(2,1)}, u32[]{:S(2)}, u32[]{:S(2)}) collective-permute-start(bf16[512,1024]{1,0:T(8,128)(2,1)S(1)} %get-tuple-element.18), channel_id=1, source_target_pairs={{0,2},{1,3},{2,0},{3,1},{4,6},{5,7},{6,4},{7,5},{8,10},{9,11},{10,... | collective-permute-start | bytes 3145736 | tf_op jit(solution)/shard_map/ppermute | solution.py:294
  111.4 52.6 %collective-permute-start.22 = (bf16[512,1024]{1,0:T(8,128)(2,1)S(1)}, bf16[512,1024]{1,0:T(8,128)(2,1)S(1)}, u32[]{:S(2)}, u32[]{:S(2)}) collective-permute-start(bf16[512,1024]{1,0:T(8,128)(2,1)S(1)} %collective-permute-done.16.refs_2_), channel_id=1, source_target_pairs={{0,1},{1,0},{2,3},{3,2},{4,5},{5,4},{6,7},{7,6},{8,9},{9,8},{10,11... | collective-permute-start | bytes 3145736 | tf_op jit(solution)/shard_map/ppermute | solution.py:294
  119.7 46.7 %collective-permute-start.21 = (bf16[512,1024]{1,0:T(8,128)(2,1)}, bf16[512,1024]{1,0:T(8,128)(2,1)S(1)}, u32[]{:S(2)}, u32[]{:S(2)}) collective-permute-start(bf16[512,1024]{1,0:T(8,128)(2,1)} %collective-permute-done.13.refs_2_), channel_id=1, source_target_pairs={{0,1},{1,0},{2,3},{3,2},{4,5},{5,4},{6,7},{7,6},{8,9},{9,8},{10,11... | collective-permute-start | bytes 3145736 | tf_op jit(solution)/shard_map/ppermute | solution.py:294
  133.9 23.7 %collective-permute-start.9 = (f32[3,256,128]{2,1,0:T(8,128)S(1)}, f32[3,256,128]{2,1,0:T(8,128)S(1)}, u32[]{:S(2)}, u32[]{:S(2)}) collective-permute-start(f32[3,256,128]{2,1,0:T(8,128)S(1)} %add.86.here_ref), channel_id=1, source_target_pairs={{0,8},{4,12},{8,0},{12,4},{1,9},{5,13},{9,1},{13,5},{2,10},{6,14},... | collective-permute-start | bytes 1179656 | tf_op jit(solution)/shard_map/ppermute | solution.py:294
  156.3 12.3 %collective-permute-start.20 = (bf16[512,1024]{1,0:T(8,128)(2,1)}, bf16[512,1024]{1,0:T(8,128)(2,1)S(1)}, u32[]{:S(2)}, u32[]{:S(2)}) collective-permute-start(bf16[512,1024]{1,0:T(8,128)(2,1)} %collective-permute-done.10.refs_2_), channel_id=1, source_target_pairs={{0,1},{1,0},{2,3},{3,2},{4,5},{5,4},{6,7},{7,6},{8,9},{9,8},{10,11... | collective-permute-start | bytes 3145736 | tf_op jit(solution)/shard_map/ppermute | solution.py:294
  157.5 12.3 %collective-permute-start.19 = (bf16[512,1024]{1,0:T(8,128)(2,1)}, bf16[512,1024]{1,0:T(8,128)(2,1)S(1)}, u32[]{:S(2)}, u32[]{:S(2)}) collective-permute-start(bf16[512,1024]{1,0:T(8,128)(2,1)} %collective-permute-done.1.refs_2_), channel_id=1, source_target_pairs={{0,1},{1,0},{2,3},{3,2},{4,5},{5,4},{6,7},{7,6},{8,9},{9,8},{10,11... | collective-permute-start | bytes 3145736 | tf_op jit(solution)/shard_map/ppermute | solution.py:294
  163.9 1.0 copy-start.8
  164.9 74.4 %collective-permute-start.26 = (bf16[3,64,5120]{2,1,0:T(8,128)(2,1)}, bf16[3,64,5120]{2,1,0:T(8,128)(2,1)}, u32[]{:S(2)}, u32[]{:S(2)}) collective-permute-start(bf16[3,64,5120]{2,1,0:T(8,128)(2,1)} %get-tuple-element.12.refs_0_), channel_id=1, source_target_pairs={{0,2},{1,3},{2,0},{3,1},{4,6},{5,7},{6,4},{7,5},{8,10},{9,11},{10,... | collective-permute-start | bytes 5898248 | tf_op jit(solution)/shard_map/ppermute | solution.py:294
  166.4 1.0 copy-start.10
  167.4 24.0 %collective-permute-start.17 = (bf16[512,1024]{1,0:T(8,128)(2,1)S(1)}, bf16[512,1024]{1,0:T(8,128)(2,1)}, u32[]{:S(2)}, u32[]{:S(2)}) collective-permute-start(bf16[512,1024]{1,0:T(8,128)(2,1)S(1)} %collective-permute-done.16.refs_2_), channel_id=1, source_target_pairs={{0,16},{16,0},{1,17},{17,1},{2,18},{18,2},{3,19},{19,3},{4,20},{20... | collective-permute-start | bytes 3145736 | tf_op jit(solution)/shard_map/ppermute | solution.py:355
  168.6 1.0 copy-start.14
  169.6 44.3 %collective-permute-start.14 = (bf16[512,1024]{1,0:T(8,128)(2,1)}, bf16[512,1024]{1,0:T(8,128)(2,1)}, u32[]{:S(2)}, u32[]{:S(2)}) collective-permute-start(bf16[512,1024]{1,0:T(8,128)(2,1)} %collective-permute-done.13.refs_2_), channel_id=1, source_target_pairs={{0,16},{16,0},{1,17},{17,1},{2,18},{18,2},{3,19},{19,3},{4,20},{20... | collective-permute-start | bytes 3145736 | tf_op jit(solution)/shard_map/ppermute | solution.py:355
  169.9 1.0 copy-start.12
  170.8 65.5 %collective-permute-start.11 = (bf16[512,1024]{1,0:T(8,128)(2,1)}, bf16[512,1024]{1,0:T(8,128)(2,1)}, u32[]{:S(2)}, u32[]{:S(2)}) collective-permute-start(bf16[512,1024]{1,0:T(8,128)(2,1)} %collective-permute-done.10.refs_2_), channel_id=1, source_target_pairs={{0,16},{16,0},{1,17},{17,1},{2,18},{18,2},{3,19},{19,3},{4,20},{20... | collective-permute-start | bytes 3145736 | tf_op jit(solution)/shard_map/ppermute | solution.py:355
  191.4 67.4 %collective-permute-start.2 = (bf16[512,1024]{1,0:T(8,128)(2,1)}, bf16[512,1024]{1,0:T(8,128)(2,1)}, u32[]{:S(2)}, u32[]{:S(2)}) collective-permute-start(bf16[512,1024]{1,0:T(8,128)(2,1)} %collective-permute-done.1.refs_2_), channel_id=1, source_target_pairs={{0,16},{16,0},{1,17},{17,1},{2,18},{18,2},{3,19},{19,3},{4,20},{20... | collective-permute-start | bytes 3145736 | tf_op jit(solution)/shard_map/ppermute | solution.py:355
  192.6 76.6 %collective-permute-start.18 = (bf16[512,1024]{1,0:T(8,128)(2,1)}, bf16[512,1024]{1,0:T(8,128)(2,1)}, u32[]{:S(2)}, u32[]{:S(2)}) collective-permute-start(bf16[512,1024]{1,0:T(8,128)(2,1)} %collective-permute-done.17.refs_2_), channel_id=1, source_target_pairs={{0,1},{1,0},{2,3},{3,2},{4,5},{5,4},{6,7},{7,6},{8,9},{9,8},{10,11... | collective-permute-start | bytes 3145736 | tf_op jit(solution)/shard_map/ppermute | solution.py:294
  196.6 1.2 copy-start.7
  197.8 1.2 copy-start.9
  199.1 37.3 %copy-start.5 = (bf16[3,64,5120]{2,1,0:T(8,128)(2,1)S(1)}, bf16[3,64,5120]{2,1,0:T(8,128)(2,1)}, u32[]{:S(2)}) copy-start(bf16[3,64,5120]{2,1,0:T(8,128)(2,1)} %get-tuple-element.12.refs_0_) | copy-start | bytes 5898244
  199.1 40.3 %copy-start.11 = (bf16[512,1024]{1,0:T(8,128)(2,1)S(1)}, bf16[512,1024]{1,0:T(8,128)(2,1)}, u32[]{:S(2)}) copy-start(bf16[512,1024]{1,0:T(8,128)(2,1)} %copy-done.10) | copy-start | bytes 3145732
  207.7 52.8 %copy-start.15 = (bf16[512,1024]{1,0:T(8,128)(2,1)S(1)}, bf16[512,1024]{1,0:T(8,128)(2,1)}, u32[]{:S(2)}) copy-start(bf16[512,1024]{1,0:T(8,128)(2,1)} %copy-done.14) | copy-start | bytes 3145732
  213.9 73.0 %collective-permute-start.15 = (bf16[512,1024]{1,0:T(8,128)(2,1)}, bf16[512,1024]{1,0:T(8,128)(2,1)S(1)}, u32[]{:S(2)}, u32[]{:S(2)}) collective-permute-start(bf16[512,1024]{1,0:T(8,128)(2,1)} %collective-permute-done.14.refs_2_), channel_id=1, source_target_pairs={{0,1},{1,0},{2,3},{3,2},{4,5},{5,4},{6,7},{7,6},{8,9},{9,8},{10,11... | collective-permute-start | bytes 3145736 | tf_op jit(solution)/shard_map/ppermute | solution.py:294
  236.4 76.7 %collective-permute-start.25 = (bf16[3,64,5120]{2,1,0:T(8,128)(2,1)S(1)}, bf16[3,64,5120]{2,1,0:T(8,128)(2,1)S(1)}, u32[]{:S(2)}, u32[]{:S(2)}) collective-permute-start(bf16[3,64,5120]{2,1,0:T(8,128)(2,1)S(1)} %copy-done.5), channel_id=1, source_target_pairs={{0,1},{1,0},{2,3},{3,2},{4,5},{5,4},{6,7},{7,6},{8,9},{9,8},{10,11... | collective-permute-start | bytes 5898248 | tf_op jit(solution)/shard_map/ppermute | solution.py:294
  239.3 73.7 %collective-permute-start.27 = (bf16[3,64,5120]{2,1,0:T(8,128)(2,1)}, bf16[3,64,5120]{2,1,0:T(8,128)(2,1)}, u32[]{:S(2)}, u32[]{:S(2)}) collective-permute-start(bf16[3,64,5120]{2,1,0:T(8,128)(2,1)} %collective-permute-done.26.refs_2_), channel_id=1, source_target_pairs={{0,1},{1,0},{2,3},{3,2},{4,5},{5,4},{6,7},{7,6},{8,9},{9,8},{10,11... | collective-permute-start | bytes 5898248 | tf_op jit(solution)/shard_map/ppermute | solution.py:294
  248.1 21.1 %copy-start.13 = (bf16[512,1024]{1,0:T(8,128)(2,1)S(1)}, bf16[512,1024]{1,0:T(8,128)(2,1)}, u32[]{:S(2)}) copy-start(bf16[512,1024]{1,0:T(8,128)(2,1)} %copy-done.12) | copy-start | bytes 3145732
  258.8 36.8 %collective-permute-start.12 = (bf16[512,1024]{1,0:T(8,128)(2,1)}, bf16[512,1024]{1,0:T(8,128)(2,1)S(1)}, u32[]{:S(2)}, u32[]{:S(2)}) collective-permute-start(bf16[512,1024]{1,0:T(8,128)(2,1)} %collective-permute-done.11.refs_2_), channel_id=1, source_target_pairs={{0,1},{1,0},{2,3},{3,2},{4,5},{5,4},{6,7},{7,6},{8,9},{9,8},{10,11... | collective-permute-start | bytes 3145736 | tf_op jit(solution)/shard_map/ppermute | solution.py:294
  269.2 35.1 %collective-permute-start.3 = (bf16[512,1024]{1,0:T(8,128)(2,1)}, bf16[512,1024]{1,0:T(8,128)(2,1)S(1)}, u32[]{:S(2)}, u32[]{:S(2)}) collective-permute-start(bf16[512,1024]{1,0:T(8,128)(2,1)} %collective-permute-done.2.refs_2_), channel_id=1, source_target_pairs={{0,1},{1,0},{2,3},{3,2},{4,5},{5,4},{6,7},{7,6},{8,9},{9,8},{10,11... | collective-permute-start | bytes 3145736 | tf_op jit(solution)/shard_map/ppermute | solution.py:294
Sparse Core Ops, SparseCore 0:
  9.6 122.0 all-gather.1

commit v2 on v1

--- a/solution.py
+++ b/solution.py
@@ -9,8 +9,14 @@
 
 adapter_scale = 2.0
 factor_gradient = 0.0625
-vmem_bytes = 50 * 1024 * 1024
+vmem_bytes = 60 * 1024 * 1024
 bf16, f32, i32 = jnp.bfloat16, jnp.float32, jnp.int32
+
+
+def behind(value, *after):
+    if not after:
+        return value
+    return lax.optimization_barrier((value, *after))[0]
 
 
 def params(cost):
@@ -163,46 +169,59 @@
     )(live, here, there, hidden, grad)
 
 
-def base_kernel(pieces, count, scalars_ref, kept_ref, *refs):
-    w_refs = refs[:pieces]
-    coef_ref, block_ref = refs[pieces : pieces + 2]
+def base_kernel(near, bounds, count, scalars_ref, kept_ref, *refs):
+    near_refs = refs[:near]
+    coef_ref, block_ref = refs[near * len(bounds) : near * len(bounds) + 2]
     out_ref = refs[-1]
-    deep = w_refs[0].shape[1]
+    deep = near_refs[0].shape[1]
     height = coef_ref.shape[1]
-    total = None
-    for r in range(pieces):
+    step = pl.program_id(0)
+
+    def part(r, w_ref):
         start = pl.multiple_of(scalars_ref[1 + r] * deep, deep)
-        part = lax.dot_general(
+        return lax.dot_general(
             kept_ref[:, pl.ds(start, deep)],
-            w_refs[r][...],
+            w_ref[...],
             (((1,), (1,)), ((), ())),
             preferred_element_type=f32,
         )
-        total = part if total is None else total + part
-    for b in range(count):
-        extra = jnp.dot(coef_ref[b], block_ref[b], preferred_element_type=f32)
-        here = total[b * height : (b + 1) * height] + extra
-        valid = lax.broadcasted_iota(i32, here.shape, 0) < scalars_ref[1 + pieces + b]
-        out_ref[b * height : (b + 1) * height, :] = jnp.where(valid, here, 0.0).astype(bf16)
-
-
-def base(scalars, kept, whole, chunk, coef, block_a, held, size, tile):
+
+    def whole_sum(far_refs):
+        total = part(0, near_refs[0])
+        for r in range(1, near):
+            total += part(r, near_refs[r])
+        for r in range(near):
+            total += part(near + r, far_refs[r])
+        for b in range(count):
+            extra = jnp.dot(coef_ref[b], block_ref[b], preferred_element_type=f32)
+            here = total[b * height : (b + 1) * height] + extra
+            valid = lax.broadcasted_iota(i32, here.shape, 0) < scalars_ref[1 + 2 * near + b]
+            out_ref[b * height : (b + 1) * height, :] = jnp.where(valid, here, 0.0).astype(bf16)
+
+    for j in range(len(bounds) - 1):
+        far_refs = refs[near * (j + 1) : near * (j + 2)]
+        pl.when((step >= bounds[j]) & (step < bounds[j + 1]))(
+            functools.partial(whole_sum, far_refs)
+        )
+
+
+def base(scalars, kept, near, chunks, coef, block_a, held, tile):
     rows, depth = kept.shape
     count, rank, ff = block_a.shape
-    pieces = len(whole) + len(chunk)
-    deep = depth // pieces
+    top = len(near)
+    deep = depth // (2 * top)
     height = rows // count
-    once2 = lambda i, s: (0, 0)
-    placed = lambda i, s: (s[0] + i, 0)
-    in_specs = [pl.BlockSpec((rows, depth), once2)]
-    operands = [kept]
-    for r in range(pieces):
-        if r in whole:
-            in_specs.append(pl.BlockSpec((tile, deep), placed))
-            operands.append(whole[r])
-        else:
-            in_specs.append(pl.BlockSpec((tile, deep), lambda i, s: (i, 0)))
-            operands.append(chunk[r])
+    bounds = [0]
+    in_specs = [pl.BlockSpec((rows, depth), lambda i, s: (0, 0))]
+    in_specs += [pl.BlockSpec((tile, deep), lambda i, s: (s[0] + i, 0))] * top
+    operands = [kept] + [near[r] for r in range(top)]
+    for chunk in chunks:
+        low = bounds[-1]
+        last = chunk[top].shape[0] // tile - 1
+        bounds.append(low + last + 1)
+        place = lambda i, s, low=low, last=last: (jnp.clip(i - low, 0, last), 0)
+        in_specs += [pl.BlockSpec((tile, deep), place)] * top
+        operands += [chunk[r] for r in range(top, 2 * top)]
     in_specs += [
         pl.BlockSpec((count, height, rank), lambda i, s: (0, 0, 0)),
         pl.BlockSpec((count, rank, tile), lambda i, s: (0, 0, s[0] + i)),
@@ -213,17 +232,18 @@
         in_specs.append(pl.BlockSpec(memory_space=pl.ANY))
         operands.append(held)
         aliases = {len(operands): 0}
+    span = bounds[-1] * tile
     return pl.pallas_call(
-        functools.partial(base_kernel, pieces, count),
+        functools.partial(base_kernel, top, bounds, count),
         grid_spec=pltpu.PrefetchScalarGridSpec(
             num_scalar_prefetch=1,
-            grid=(size // tile,),
+            grid=(bounds[-1],),
             in_specs=in_specs,
             out_specs=pl.BlockSpec((rows, tile), lambda i, s: (0, s[0] + i)),
         ),
         out_shape=jax.ShapeDtypeStruct((rows, ff), bf16),
         input_output_aliases=aliases,
-        **params((2 * rows * depth * size, 2 * (rows * depth + (rows + depth) * size))),
+        **params((2 * rows * depth * span, 2 * (rows * depth + (rows + depth) * span))),
     )(scalars, *operands)
 
 
@@ -308,72 +328,102 @@
 
     kept = lax.all_gather(output_gradient, "fsdp", axis=1, tiled=True)
 
+    share = ff // n_groups
+    unit = share // 8 if share % 2048 == 0 else share
+    sizes = [unit, 2 * unit, 2 * unit, 2 * unit, unit] if unit < share else [share]
+    tile = min(256, unit)
+    starts = [sum(sizes[:j]) for j in range(len(sizes))]
+    crossed, turned = [], []
+
+    def cross(*after):
+        j = len(crossed)
+        if j == len(sizes):
+            return
+        piece = lax.dynamic_slice_in_dim(
+            frozen_down_weight, group * share + starts[j], sizes[j], axis=0
+        )
+        crossed.append(swap(behind(piece, *after), top))
+
+    def turn(*after):
+        j = len(turned)
+        if j == len(sizes):
+            return
+        turned.append(
+            [
+                lax.ppermute(
+                    behind(crossed[j], *after),
+                    "groups",
+                    [(i, (i + shift) % n_groups) for i in range(n_groups)],
+                )
+                for shift in range(1, n_groups)
+            ]
+        )
+
+    cross()
+
     first = jnp.swapaxes(adapter_first_factors, 1, 2)
     a_near = spread({0: first})
     b_near = spread({0: adapter_second_factors})
     near = sorted(a_near)
     a_near = [a_near[r] for r in near]
     b_near = [b_near[r] for r in near]
+    whole = spread({0: frozen_down_weight})
 
     def places(wanted):
         owner = wanted // local
         index = jnp.concatenate([wanted % local] * len(near))
         return index, jnp.where((owner ^ me) < top, owner ^ me, len(near))
 
-    far = swap(pick(*places(far_slots), a_near, b_near), top)
-
-    share = ff // n_groups
-    size = max(min(share, 256), share // 4)
-    tile = min(512, size)
-    shares = []
-    for j in range(share // size):
-        shares.append(
-            swap(
-                lax.dynamic_slice_in_dim(
-                    frozen_down_weight, group * share + j * size, size, axis=0
-                ),
-                top,
-            )
-        )
-    whole = spread({0: frozen_down_weight})
-
-    part, block_a = project(*places(slots), a_near, b_near, far, hidden, output_gradient)
+    far = swap(pick(*places(behind(far_slots, *crossed)), a_near, b_near), top)
+    both_slots = spread({0: jnp.concatenate([slots, far_slots])})
+    cross(far)
+    turn()
+
+    ready = behind(slots, *whole.values(), *turned[0], *both_slots.values())
+    part, block_a = project(*places(ready), a_near, b_near, far, hidden, output_gradient)
+    cross(part)
+    turn(part)
     bit = 1
     total = None
     while bit < n_fsdp:
         total = part if total is None else total + other
         other = swap(total, bit, "fsdp", n_fsdp)
         bit *= 2
-    terms, coef = block_terms(island_live_rows, total, other, hidden, output_gradient)
+    cross(total, *crossed[:2])
+    live = behind(island_live_rows, *crossed[:2], *sum(turned[:1], []))
+    terms, coef = block_terms(live, total, other, hidden, output_gradient)
     far_terms = swap(terms, top)
+    cross(terms, *crossed[:3])
+    turn(total)
+    turn(terms)
+    turn(terms)
 
     order = [me ^ r for r in range(n_dp)]
     grad_hidden = None
     for shift in range(n_groups):
-        for j, piece in enumerate(shares):
-            if shift:
-                piece = lax.ppermute(
-                    piece, "groups", [(i, (i + shift) % n_groups) for i in range(n_groups)]
-                )
-            start = lax.rem(group + n_groups - shift, n_groups) * share + j * size
-            scalars = jnp.stack([start // tile] + order).astype(i32)
+        pieces = [
+            spread({top: turned[j][shift - 1] if shift else crossed[j]}) for j in range(len(sizes))
+        ]
+        start = lax.rem(group + n_groups - shift, n_groups) * share
+        cuts = [0, len(sizes)] if shift == 0 or len(sizes) == 1 else [0, len(sizes) - 1, len(sizes)]
+        for low, high in zip(cuts, cuts[1:]):
+            scalars = jnp.stack([(start + starts[low]) // tile] + order).astype(i32)
             grad_hidden = base(
                 jnp.concatenate([scalars, island_live_rows]),
                 kept,
                 whole,
-                spread({top: piece}),
+                pieces[low:high],
                 coef,
                 block_a,
                 grad_hidden,
-                size,
                 tile,
             )
 
-    all_slots = spread({0: slots, top: far_slots})
     all_terms = spread({0: terms, top: far_terms})
     keys = sorted(all_terms)
-    relative = jnp.concatenate([all_slots[r] for r in keys]) - me * local
-    grad_a, grad_b = merge(relative, [all_terms[r] for r in keys], local, ff, min(d, 512))
+    relative = [both_slots[r][:count] for r in near] + [both_slots[r][count:] for r in near]
+    relative = jnp.concatenate(relative) - me * local
+    grad_a, grad_b = merge(relative, [all_terms[r] for r in keys], local, ff, d)
     return grad_hidden, jnp.swapaxes(grad_a, 1, 2), grad_b
 
 

time: 333 us -> 311 us (0.934)
  Pallas kernels: 96.6 us -> 80.1 us
  local copies, waits for them, and re-layouts: 13.9 us -> 9.36 us
  starting transfers between devices: 30.9 us -> 27 us
  other arithmetic: 1.16 us -> 4.99 us
    ppermute x4 -> x5, waiting for transfers between devices: 55.8 us -> 20 us  [turn(): lax.ppermute(behind(crossed[j], *after), 'groups', [(i, (i + shift) % n_g...]
    ppermute x24 -> x26, waiting for transfers between devices: 117 us -> 152 us  [swap(): return lax.ppermute(value, axis, [(i, i ^ bit) for i in range(size)])]
    pallas_call x8 -> x3, Pallas kernels: 69.8 us -> 50.4 us  [base(): pl.pallas_call(functools.partial(base_kernel, top, bounds, count), grid_s...]
    unnamed x34 -> x24, local copies, waits for them, and re-layouts: 10.6 us -> 1.63 us
    ppermute x24 -> x26, starting transfers between devices: 27 us -> 22.3 us  [swap(): return lax.ppermute(value, axis, [(i, i ^ bit) for i in range(size)])]
  transfers between devices with their start and end apart: 29 -> 32, of which waited for: 13 -> 9; matrix products, arithmetic and copies ran while one was open for 1% -> 4% of each run, Pallas kernels for 26% -> 23%
where the time goes in v2:
time: 311 us; the launch traced here: 308 us
  waiting for transfers between devices  172 us (55%)
  Pallas kernels  80.1 us (26%)
  starting transfers between devices  27 us (9%)
  between operations  14.2 us (5%)
  local copies, waits for them, and re-layouts  9.36 us (3%)
  other arithmetic  4.99 us (2%)
    ppermute x26, waiting for transfers between devices, swap(): return lax.ppermute(value, axis, [(i, i ^ bit) for i in range(size)])  152 us
    pallas_call x3, Pallas kernels, base(): pl.pallas_call(functools.partial(base_kernel, top, bounds, count), grid_s...  50.4 us
    ppermute x26, starting transfers between devices, swap(): return lax.ppermute(value, axis, [(i, i ^ bit) for i in range(size)])  22.3 us
    ppermute x5, waiting for transfers between devices, turn(): lax.ppermute(behind(crossed[j], *after), 'groups', [(i, (i + shift) % n_g...  20 us
    pallas_call x1, Pallas kernels, merge(): pl.pallas_call(functools.partial(merge_kernel, len(pieces), count, tiles)...  9.76 us
    pallas_call x1, Pallas kernels, project(): pl.pallas_call(functools.partial(project_kernel, pieces), grid_spec=pltpu...  8.07 us
    pallas_call x1, Pallas kernels, block_terms(): pl.pallas_call(terms_kernel, grid_spec=pltpu.PrefetchScalarGridSpec(num_s...  7.01 us
  transfers between devices with their start and end apart: 32, of which 9 were waited for; matrix products, arithmetic and copies ran while one was open for 4% of the time, Pallas kernels for 23%

profile of v2, /device:TPU:11, one launch (start us, length us, event | category | flops | bytes accessed | tf_op | source)
XLA Modules:
  0.0 307.9 jit_solution(5778351483788799478)
XLA Ops:
  7.2 0.0 all-gather.2.cloned.1.call-start
  7.2 0.7 collective-permute-start
  8.0 0.1 collective-permute-start.3
  8.1 0.6 collective-permute-start.4
  8.6 2.1 constant_dynamic-slice_fusion.3
  10.8 0.3 collective-permute-start.1
  11.0 0.9 select_reduce_fusion
  11.9 1.3 collective-permute-start.2
  13.1 11.2 %collective-permute-done.2 = s32[3]{0:T(128)S(1)} collective-permute-done((s32[3]{0:T(128)S(1)}, s32[3]{0:T(128)S(1)}, u32[]{:S(2)}, u32[]{:S(2)}) %collective-permute-start.2) | collective-permute-done | bytes 44 | tf_op jit(solution)/shard_map/ppermute | solution.py:314
  24.4 0.5 compare_select_fusion.1
  24.9 0.6 pad_add_fusion.index_ref
  25.6 3.0 collective-permute-done.3.refs_1_
  28.6 4.8 %shard_map.103 = bf16[3,64,5120]{2,1,0:T(8,128)(2,1)} custom-call(s32[6]{0:T(128)} %pad_add_fusion.index_ref, s32[3]{0:T(128)} %get-tuple-element.46.source_ref, bf16[8,64,4096]{2,1,0:T(8,128)(2,1)} %bitcast.10, bf16[8,64,4096]{2,1,0:T(8,128)(2,1)} %collective-permute-done.3.refs_1_, bf16[8,64,1024]{2,1,0:T(8,128)(2,1)} %refs_2_.3, bf16[8,64,1024]{2,1,0:T(8,128)(2,1)} %copy-done), custom_call_target="tpu_custom_call" | custom-call | bytes 5898240 | tf_op jit(solution)/shard_map/pallas_call | solution.py:54
  33.4 0.3 collective-permute-start.5
  33.6 1.2 collective-permute-start.7
  34.9 3.6 %constant_dynamic-slice_fusion = (bf16[512,1024]{1,0:T(8,128)(2,1)}, bf16[512,1024]{1,0:T(8,128)(2,1)S(1)}, bf16[512,1024]{1,0:T(8,128)(2,1)}) fusion(bf16[4096,1024]{1,0:T(8,128)(2,1)} %refs_0_.5, s32[]{:T(128)S(6)} %select_n.68, s32[]{:T(128)S(6)} %select_n.66, s32[]{:T(128)S(6)} %select_n.58), kind=kLoop, calls=%fused_computation.7 | loop fusion | bytes 6291468 | tf_op jit(solution)/shard_map/dynamic_slice | solution.py:342
  38.5 39.2 %collective-permute-done.5.refs_4_ = bf16[3,64,5120]{2,1,0:T(8,128)(2,1)S(1)} collective-permute-done((bf16[3,64,5120]{2,1,0:T(8,128)(2,1)}, bf16[3,64,5120]{2,1,0:T(8,128)(2,1)S(1)}, u32[]{:S(2)}, u32[]{:S(2)}) %collective-permute-start.5) | collective-permute-done | bytes 1966112 | tf_op jit(solution)/shard_map/ppermute | solution.py:314
  77.7 0.3 collective-permute-start.6
  78.0 0.1 pad_add_fusion.1
  78.0 1.4 collective-permute-start.8
  79.4 0.8 collective-permute-done.8
  80.2 0.6 compare_select_fusion
  80.8 0.7 pad_add_fusion.2.index_ref
  81.5 8.1 %shard_map.104 = (f32[3,256,128]{2,1,0:T(8,128)}, bf16[3,64,4096]{2,1,0:T(8,128)(2,1)}) custom-call(s32[6]{0:T(128)} %pad_add_fusion.2.index_ref, s32[3]{0:T(128)} %get-tuple-element.44.source_ref, bf16[8,64,4096]{2,1,0:T(8,128)(2,1)} %bitcast.11, bf16[8,64,4096]{2,1,0:T(8,128)(2,1)} %collective-permute-done.3.refs_1_, bf16[8,64,1024]{2,1,0:T(8,128)(2,1)} %refs_2_.3, ...), custom_call_target="tpu_custom_call" | custom-call | flops 503316480 | bytes 15728640 | tf_op jit(solution)/shard_map/pallas_call | solution.py:95
  89.6 1.2 collective-permute-start.11
  90.8 0.6 collective-permute-start.23
  91.4 0.2 collective-permute-start.9
  91.5 10.0 %collective-permute-done.6.refs_4_ = bf16[512,1024]{1,0:T(8,128)(2,1)} collective-permute-done((bf16[512,1024]{1,0:T(8,128)(2,1)}, bf16[512,1024]{1,0:T(8,128)(2,1)}, u32[]{:S(2)}, u32[]{:S(2)}) %collective-permute-start.6) | collective-permute-done | bytes 1048608 | tf_op jit(solution)/shard_map/ppermute | solution.py:314
  101.6 3.6 %collective-permute-start.24 = (bf16[512,1024]{1,0:T(8,128)(2,1)}, bf16[512,1024]{1,0:T(8,128)(2,1)}, u32[]{:S(2)}, u32[]{:S(2)}) collective-permute-start(bf16[512,1024]{1,0:T(8,128)(2,1)} %collective-permute-done.6.refs_4_), channel_id=1, source_target_pairs={{0,1},{1,0},{2,3},{3,2},{4,5},{5,4},{6,7},{7,6},{8,9},{9,8},{10,11... | collective-permute-start | bytes 3145736 | tf_op jit(solution)/shard_map/ppermute | solution.py:314
  105.2 0.8 collective-permute-start.16
  106.0 19.7 %collective-permute-done.9 = f32[3,256,128]{2,1,0:T(8,128)S(1)} collective-permute-done((f32[3,256,128]{2,1,0:T(8,128)}, f32[3,256,128]{2,1,0:T(8,128)S(1)}, u32[]{:S(2)}, u32[]{:S(2)}) %collective-permute-start.9) | collective-permute-done | bytes 393248 | tf_op jit(solution)/shard_map/ppermute | solution.py:314
  125.8 1.0 add.71.here_ref
  126.8 3.9 %collective-permute-start.10 = (f32[3,256,128]{2,1,0:T(8,128)S(1)}, f32[3,256,128]{2,1,0:T(8,128)S(1)}, u32[]{:S(2)}, u32[]{:S(2)}) collective-permute-start(f32[3,256,128]{2,1,0:T(8,128)S(1)} %add.71.here_ref), channel_id=1, source_target_pairs={{0,8},{4,12},{8,0},{12,4},{1,9},{5,13},{9,1},{13,5},{2,10},{6,14},... | collective-permute-start | bytes 1179656 | tf_op jit(solution)/shard_map/ppermute | solution.py:314
  130.7 0.6 collective-permute-start.15
  131.3 0.1 collective-permute-start.20
  131.4 16.0 %collective-permute-done.10.there_ref = f32[3,256,128]{2,1,0:T(8,128)S(1)} collective-permute-done((f32[3,256,128]{2,1,0:T(8,128)S(1)}, f32[3,256,128]{2,1,0:T(8,128)S(1)}, u32[]{:S(2)}, u32[]{:S(2)}) %collective-permute-start.10) | collective-permute-done | bytes 393248 | tf_op jit(solution)/shard_map/ppermute | solution.py:314
  147.3 1.1 collective-permute-start.18
  148.5 7.0 %shard_map.105 = (bf16[3,64,5120]{2,1,0:T(8,128)(2,1)}, bf16[3,256,64]{2,1,0:T(8,128)(2,1)}) custom-call(s32[3]{0:T(128)} %live_ref, f32[3,256,128]{2,1,0:T(8,128)} %copy-done.3, f32[3,256,128]{2,1,0:T(8,128)} %copy-done.9, bf16[768,4096]{1,0:T(8,128)(2,1)} %hid_ref.1, bf16[768,1024]{1,0:T(8,128)(2,1)} %grad_ref.1), custom_call_target="tpu_custom_call" | custom-call | flops 503316480 | bytes 9830400 | tf_op jit(solution)/shard_map/pallas_call | solution.py:148
  155.5 0.8 copy-done.6
  156.3 0.3 collective-permute-start.29
  156.7 1.0 collective-permute-start.25
  157.7 1.2 collective-permute-start.12
  158.9 0.3 collective-permute-start.17
  159.2 52.2 %collective-permute-done.12.refs_10_ = bf16[256,1024]{1,0:T(8,128)(2,1)} collective-permute-done((bf16[256,1024]{1,0:T(8,128)(2,1)}, bf16[256,1024]{1,0:T(8,128)(2,1)}, u32[]{:S(2)}, u32[]{:S(2)}) %collective-permute-start.12) | collective-permute-done | bytes 524320 | tf_op jit(solution)/shard_map/ppermute | solution.py:314
  211.4 1.7 collective-permute-start.26
  213.1 0.7 collective-permute-start.21
  213.8 0.3 collective-permute-start.27
  214.1 0.6 concatenate.21.scalars_ref
  214.8 0.7 concatenate.26.scalars_ref
  215.4 0.6 concatenate.25.scalars_ref
  216.0 0.1 fusion
  216.1 0.6 add_subtract_fusion.slots_ref
  216.7 0.2 collective-permute-start.28
  216.9 0.7 collective-permute-start.13
  217.7 0.6 collective-permute-start.19
  218.2 20.0 %collective-permute-done.21.refs_8_ = bf16[512,1024]{1,0:T(8,128)(2,1)} collective-permute-done((bf16[512,1024]{1,0:T(8,128)(2,1)}, bf16[512,1024]{1,0:T(8,128)(2,1)}, u32[]{:S(2)}, u32[]{:S(2)}) %collective-permute-start.21) | collective-permute-done | bytes 1048608 | tf_op jit(solution)/shard_map/ppermute | solution.py:353
  238.2 1.2 collective-permute-start.22
  239.4 0.1 collective-permute-start.30
  239.5 23.0 %shard_map.106.refs_12_ = bf16[768,4096]{1,0:T(8,128)(2,1)} custom-call(s32[8]{0:T(128)} %concatenate.26.scalars_ref, bf16[768,4096]{1,0:T(8,128)(2,1)} %all-gather.2.cloned.1.call-done.kept_ref, bf16[4096,1024]{1,0:T(8,128)(2,1)} %refs_0_.5, bf16[4096,1024]{1,0:T(8,128)(2,1)} %collective-permute-done.refs_1_, ...), custom_call_target="tpu_custom_call" | custom-call | flops 12884901888 | bytes 26214400 | tf_op jit(solution)/shard_map/pallas_call | solution.py:236
  262.5 0.5 collective-permute-start.14
  263.0 20.8 %shard_map.107.refs_6_ = bf16[768,4096]{1,0:T(8,128)(2,1)} custom-call(s32[8]{0:T(128)} %concatenate.25.scalars_ref, bf16[768,4096]{1,0:T(8,128)(2,1)} %all-gather.2.cloned.1.call-done.kept_ref, bf16[4096,1024]{1,0:T(8,128)(2,1)} %refs_0_.5, bf16[4096,1024]{1,0:T(8,128)(2,1)} %collective-permute-done.refs_1_, ...), custom_call_target="tpu_custom_call", output_to_operand_aliasing={{}: (14, {})} | custom-call | flops 11274289152 | bytes 23724032 | tf_op jit(solution)/shard_map/pallas_call | solution.py:236
  283.8 0.8 copy-done.8
  284.6 6.7 %shard_map.108 = bf16[768,4096]{1,0:T(8,128)(2,1)} custom-call(s32[8]{0:T(128)} %concatenate.21.scalars_ref, bf16[768,4096]{1,0:T(8,128)(2,1)} %all-gather.2.cloned.1.call-done.kept_ref, bf16[4096,1024]{1,0:T(8,128)(2,1)} %refs_0_.5, bf16[4096,1024]{1,0:T(8,128)(2,1)} %collective-permute-done.refs_1_, ...), custom_call_target="tpu_custom_call", output_to_operand_aliasing={{}: (8, {})} | custom-call | flops 1610612736 | bytes 8781824 | tf_op jit(solution)/shard_map/pallas_call | solution.py:236
  291.3 9.8 %shard_map.109 = (f32[8,64,4096]{2,1,0:T(8,128)}, f32[8,64,1024]{2,1,0:T(8,128)}) custom-call(s32[12]{0:T(128)} %add_subtract_fusion.slots_ref, bf16[3,64,5120]{2,1,0:T(8,128)(2,1)} %get-tuple-element.25.refs_0_, bf16[3,64,5120]{2,1,0:T(8,128)(2,1)} %collective-permute-done.28.refs_1_, bf16[3,64,5120]{2,1,0:T(8,128)(2,1)} %copy-done.2, ...), custom_call_target="tpu_custom_call" | custom-call | bytes 18350080 | tf_op jit(solution)/shard_map/pallas_call | solution.py:272
  (46 shorter events, 0.1 us)
Async XLA Ops:
  7.2 232.3 %all-gather.2.cloned.1.call-start = ((), (), s32[]{:S(2)}) async-start(), calls=%async_computation | async-start | bytes 7864320 | tf_op jit(solution)/shard_map/all_gather | solution.py:329
  7.2 73.0 %collective-permute-start = (bf16[4096,1024]{1,0:T(8,128)(2,1)}, bf16[4096,1024]{1,0:T(8,128)(2,1)}, u32[]{:S(2)}, u32[]{:S(2)}) collective-permute-start(bf16[4096,1024]{1,0:T(8,128)(2,1)} %refs_0_.5), channel_id=1, source_target_pairs={{0,1},{1,0},{2,3},{3,2},{4,5},{5,4},{6,7},{7,6},{8,9},{9,8},{10,11... | collective-permute-start | bytes 25165832 | tf_op jit(solution)/shard_map/ppermute | solution.py:314
  8.0 20.6 %collective-permute-start.3 = (bf16[8,64,4096]{2,1,0:T(8,128)(2,1)}, bf16[8,64,4096]{2,1,0:T(8,128)(2,1)}, u32[]{:S(2)}, u32[]{:S(2)}) collective-permute-start(bf16[8,64,4096]{2,1,0:T(8,128)(2,1)} %bitcast.9), channel_id=1, source_target_pairs={{0,1},{1,0},{2,3},{3,2},{4,5},{5,4},{6,7},{7,6},{8,9},{9,8},{10,11... | collective-permute-start | bytes 12582920 | tf_op jit(solution)/shard_map/ppermute | solution.py:314
  8.1 17.5 %collective-permute-start.4 = (bf16[8,64,1024]{2,1,0:T(8,128)(2,1)}, bf16[8,64,1024]{2,1,0:T(8,128)(2,1)S(1)}, u32[]{:S(2)}, u32[]{:S(2)}) collective-permute-start(bf16[8,64,1024]{2,1,0:T(8,128)(2,1)} %refs_2_.3), channel_id=1, source_target_pairs={{0,1},{1,0},{2,3},{3,2},{4,5},{5,4},{6,7},{7,6},{8,9},{9,8},{10,11... | collective-permute-start | bytes 3145736 | tf_op jit(solution)/shard_map/ppermute | solution.py:314
  10.8 13.6 %collective-permute-start.1 = (bf16[256,1024]{1,0:T(8,128)(2,1)S(1)}, bf16[256,1024]{1,0:T(8,128)(2,1)}, u32[]{:S(2)}, u32[]{:S(2)}) collective-permute-start(bf16[256,1024]{1,0:T(8,128)(2,1)S(1)} %get-tuple-element.40), channel_id=1, source_target_pairs={{0,2},{1,3},{2,0},{3,1},{4,6},{5,7},{6,4},{7,5},{8,10},{9,11},{10,... | collective-permute-start | bytes 1572872 | tf_op jit(solution)/shard_map/ppermute | solution.py:314
  11.9 12.5 %collective-permute-start.2 = (s32[3]{0:T(128)S(1)}, s32[3]{0:T(128)S(1)}, u32[]{:S(2)}, u32[]{:S(2)}) collective-permute-start(s32[3]{0:T(128)S(1)} %select_reduce_fusion), channel_id=1, source_target_pairs={{0,2},{1,3},{2,0},{3,1},{4,6},{5,7},{6,4},{7,5},{8,10},{9,11},{10,... | collective-permute-start | bytes 44 | tf_op jit(solution)/shard_map/ppermute | solution.py:314
  25.6 3.0 copy-start
  33.4 44.3 %collective-permute-start.5 = (bf16[3,64,5120]{2,1,0:T(8,128)(2,1)}, bf16[3,64,5120]{2,1,0:T(8,128)(2,1)S(1)}, u32[]{:S(2)}, u32[]{:S(2)}) collective-permute-start(bf16[3,64,5120]{2,1,0:T(8,128)(2,1)} %shard_map.103), channel_id=1, source_target_pairs={{0,2},{1,3},{2,0},{3,1},{4,6},{5,7},{6,4},{7,5},{8,10},{9,11},{10,... | collective-permute-start | bytes 5898248 | tf_op jit(solution)/shard_map/ppermute | solution.py:314
  33.6 46.6 %collective-permute-start.7 = (bf16[256,1024]{1,0:T(8,128)(2,1)}, bf16[256,1024]{1,0:T(8,128)(2,1)S(1)}, u32[]{:S(2)}, u32[]{:S(2)}) collective-permute-start(bf16[256,1024]{1,0:T(8,128)(2,1)} %collective-permute-done.1.refs_2_), channel_id=1, source_target_pairs={{0,16},{16,0},{1,17},{17,1},{2,18},{18,2},{3,19},{19,3},{4,20},{20... | collective-permute-start | bytes 1572872 | tf_op jit(solution)/shard_map/ppermute | solution.py:353
  77.7 3.8 %copy-start.1 = (bf16[3,64,5120]{2,1,0:T(8,128)(2,1)}, bf16[3,64,5120]{2,1,0:T(8,128)(2,1)S(1)}, u32[]{:S(2)}) copy-start(bf16[3,64,5120]{2,1,0:T(8,128)(2,1)S(1)} %collective-permute-done.5.refs_4_) | copy-start | bytes 5898244
  77.7 23.9 %collective-permute-start.6 = (bf16[512,1024]{1,0:T(8,128)(2,1)}, bf16[512,1024]{1,0:T(8,128)(2,1)}, u32[]{:S(2)}, u32[]{:S(2)}) collective-permute-start(bf16[512,1024]{1,0:T(8,128)(2,1)} %get-tuple-element.21), channel_id=1, source_target_pairs={{0,2},{1,3},{2,0},{3,1},{4,6},{5,7},{6,4},{7,5},{8,10},{9,11},{10,... | collective-permute-start | bytes 3145736 | tf_op jit(solution)/shard_map/ppermute | solution.py:314
  78.0 2.2 collective-permute-start.8
  80.2 50.5 %copy-start.5 = (bf16[256,1024]{1,0:T(8,128)(2,1)}, bf16[256,1024]{1,0:T(8,128)(2,1)S(1)}, u32[]{:S(2)}) copy-start(bf16[256,1024]{1,0:T(8,128)(2,1)S(1)} %collective-permute-done.7.refs_2_) | copy-start | bytes 1572868
  89.6 41.7 %collective-permute-start.11 = (bf16[512,1024]{1,0:T(8,128)(2,1)S(1)}, bf16[512,1024]{1,0:T(8,128)(2,1)}, u32[]{:S(2)}, u32[]{:S(2)}) collective-permute-start(bf16[512,1024]{1,0:T(8,128)(2,1)S(1)} %get-tuple-element.26), channel_id=1, source_target_pairs={{0,2},{1,3},{2,0},{3,1},{4,6},{5,7},{6,4},{7,5},{8,10},{9,11},{10,... | collective-permute-start | bytes 3145736 | tf_op jit(solution)/shard_map/ppermute | solution.py:314
  90.8 39.9 %collective-permute-start.23 = (bf16[256,1024]{1,0:T(8,128)(2,1)}, bf16[256,1024]{1,0:T(8,128)(2,1)S(1)}, u32[]{:S(2)}, u32[]{:S(2)}) collective-permute-start(bf16[256,1024]{1,0:T(8,128)(2,1)} %collective-permute-done.1.refs_2_), channel_id=1, source_target_pairs={{0,1},{1,0},{2,3},{3,2},{4,5},{5,4},{6,7},{7,6},{8,9},{9,8},{10,11... | collective-permute-start | bytes 1572872 | tf_op jit(solution)/shard_map/ppermute | solution.py:314
  91.4 34.4 %collective-permute-start.9 = (f32[3,256,128]{2,1,0:T(8,128)}, f32[3,256,128]{2,1,0:T(8,128)S(1)}, u32[]{:S(2)}, u32[]{:S(2)}) collective-permute-start(f32[3,256,128]{2,1,0:T(8,128)} %get-tuple-element.24), channel_id=1, source_target_pairs={{0,4},{4,0},{8,12},{12,8},{1,5},{5,1},{9,13},{13,9},{2,6},{6,2},{1... | collective-permute-start | bytes 1179656 | tf_op jit(solution)/shard_map/ppermute | solution.py:314
  101.6 55.1 %collective-permute-start.24 = (bf16[512,1024]{1,0:T(8,128)(2,1)}, bf16[512,1024]{1,0:T(8,128)(2,1)}, u32[]{:S(2)}, u32[]{:S(2)}) collective-permute-start(bf16[512,1024]{1,0:T(8,128)(2,1)} %collective-permute-done.6.refs_4_), channel_id=1, source_target_pairs={{0,1},{1,0},{2,3},{3,2},{4,5},{5,4},{6,7},{7,6},{8,9},{9,8},{10,11... | collective-permute-start | bytes 3145736 | tf_op jit(solution)/shard_map/ppermute | solution.py:314
  105.2 52.5 %collective-permute-start.16 = (bf16[512,1024]{1,0:T(8,128)(2,1)}, bf16[512,1024]{1,0:T(8,128)(2,1)S(1)}, u32[]{:S(2)}, u32[]{:S(2)}) collective-permute-start(bf16[512,1024]{1,0:T(8,128)(2,1)} %collective-permute-done.6.refs_4_), channel_id=1, source_target_pairs={{0,16},{16,0},{1,17},{17,1},{2,18},{18,2},{3,19},{19,3},{4,20},{20... | collective-permute-start | bytes 3145736 | tf_op jit(solution)/shard_map/ppermute | solution.py:353
  126.8 21.7 %copy-start.3 = (f32[3,256,128]{2,1,0:T(8,128)}, f32[3,256,128]{2,1,0:T(8,128)S(1)}, u32[]{:S(2)}) copy-start(f32[3,256,128]{2,1,0:T(8,128)S(1)} %add.71.here_ref) | copy-start | bytes 1179652
  126.8 20.5 %collective-permute-start.10 = (f32[3,256,128]{2,1,0:T(8,128)S(1)}, f32[3,256,128]{2,1,0:T(8,128)S(1)}, u32[]{:S(2)}, u32[]{:S(2)}) collective-permute-start(f32[3,256,128]{2,1,0:T(8,128)S(1)} %add.71.here_ref), channel_id=1, source_target_pairs={{0,8},{4,12},{8,0},{12,4},{1,9},{5,13},{9,1},{13,5},{2,10},{6,14},... | collective-permute-start | bytes 1179656 | tf_op jit(solution)/shard_map/ppermute | solution.py:314
  130.7 16.6 %copy-start.11 = (bf16[256,1024]{1,0:T(8,128)(2,1)}, bf16[256,1024]{1,0:T(8,128)(2,1)S(1)}, u32[]{:S(2)}) copy-start(bf16[256,1024]{1,0:T(8,128)(2,1)S(1)} %collective-permute-done.23.refs_3_) | copy-start | bytes 1572868
  130.7 24.8 %collective-permute-start.15 = (bf16[256,1024]{1,0:T(8,128)(2,1)S(1)}, bf16[256,1024]{1,0:T(8,128)(2,1)S(1)}, u32[]{:S(2)}, u32[]{:S(2)}) collective-permute-start(bf16[256,1024]{1,0:T(8,128)(2,1)S(1)} %collective-permute-done.7.refs_2_), channel_id=1, source_target_pairs={{0,1},{1,0},{2,3},{3,2},{4,5},{5,4},{6,7},{7,6},{8,9},{9,8},{10,11... | collective-permute-start | bytes 1572872 | tf_op jit(solution)/shard_map/ppermute | solution.py:314
  131.3 82.8 %copy-start.10 = (s32[3]{0:T(128)S(1)}, s32[3]{0:T(128)}, u32[]{:S(2)}) copy-start(s32[3]{0:T(128)} %live_ref) | copy-start | bytes 40
  131.3 27.5 %collective-permute-start.20 = (bf16[512,1024]{1,0:T(8,128)(2,1)}, bf16[512,1024]{1,0:T(8,128)(2,1)}, u32[]{:S(2)}, u32[]{:S(2)}) collective-permute-start(bf16[512,1024]{1,0:T(8,128)(2,1)} %get-tuple-element.33), channel_id=1, source_target_pairs={{0,2},{1,3},{2,0},{3,1},{4,6},{5,7},{6,4},{7,5},{8,10},{9,11},{10,... | collective-permute-start | bytes 3145736 | tf_op jit(solution)/shard_map/ppermute | solution.py:314
  147.3 1.1 copy-start.9
  147.3 65.8 %collective-permute-start.18 = (bf16[512,1024]{1,0:T(8,128)(2,1)}, bf16[512,1024]{1,0:T(8,128)(2,1)}, u32[]{:S(2)}, u32[]{:S(2)}) collective-permute-start(bf16[512,1024]{1,0:T(8,128)(2,1)} %collective-permute-done.11.refs_6_), channel_id=1, source_target_pairs={{0,16},{16,0},{1,17},{17,1},{2,18},{18,2},{3,19},{19,3},{4,20},{20... | collective-permute-start | bytes 3145736 | tf_op jit(solution)/shard_map/ppermute | solution.py:353
  155.5 0.8 copy-start.6
  156.3 83.1 %collective-permute-start.29 = (bf16[3,64,5120]{2,1,0:T(8,128)(2,1)}, bf16[3,64,5120]{2,1,0:T(8,128)(2,1)S(1)}, u32[]{:S(2)}, u32[]{:S(2)}) collective-permute-start(bf16[3,64,5120]{2,1,0:T(8,128)(2,1)} %get-tuple-element.25.refs_0_), channel_id=1, source_target_pairs={{0,2},{1,3},{2,0},{3,1},{4,6},{5,7},{6,4},{7,5},{8,10},{9,11},{10,... | collective-permute-start | bytes 5898248 | tf_op jit(solution)/shard_map/ppermute | solution.py:314
  156.7 57.2 %collective-permute-start.25 = (bf16[512,1024]{1,0:T(8,128)(2,1)}, bf16[512,1024]{1,0:T(8,128)(2,1)}, u32[]{:S(2)}, u32[]{:S(2)}) collective-permute-start(bf16[512,1024]{1,0:T(8,128)(2,1)} %collective-permute-done.11.refs_6_), channel_id=1, source_target_pairs={{0,1},{1,0},{2,3},{3,2},{4,5},{5,4},{6,7},{7,6},{8,9},{9,8},{10,11... | collective-permute-start | bytes 3145736 | tf_op jit(solution)/shard_map/ppermute | solution.py:314
  157.7 104.8 %copy-start.4 = (bf16[512,1024]{1,0:T(8,128)(2,1)}, bf16[512,1024]{1,0:T(8,128)(2,1)S(1)}, u32[]{:S(2)}) copy-start(bf16[512,1024]{1,0:T(8,128)(2,1)S(1)} %collective-permute-done.16.refs_4_) | copy-start | bytes 3145732
  157.7 53.7 %collective-permute-start.12 = (bf16[256,1024]{1,0:T(8,128)(2,1)}, bf16[256,1024]{1,0:T(8,128)(2,1)}, u32[]{:S(2)}, u32[]{:S(2)}) collective-permute-start(bf16[256,1024]{1,0:T(8,128)(2,1)} %get-tuple-element.27), channel_id=1, source_target_pairs={{0,2},{1,3},{2,0},{3,1},{4,6},{5,7},{6,4},{7,5},{8,10},{9,11},{10,... | collective-permute-start | bytes 1572872 | tf_op jit(solution)/shard_map/ppermute | solution.py:314
  158.9 57.8 %collective-permute-start.17 = (bf16[512,1024]{1,0:T(8,128)(2,1)S(1)}, bf16[512,1024]{1,0:T(8,128)(2,1)}, u32[]{:S(2)}, u32[]{:S(2)}) collective-permute-start(bf16[512,1024]{1,0:T(8,128)(2,1)S(1)} %collective-permute-done.16.refs_4_), channel_id=1, source_target_pairs={{0,1},{1,0},{2,3},{3,2},{4,5},{5,4},{6,7},{7,6},{8,9},{9,8},{10,11... | collective-permute-start | bytes 3145736 | tf_op jit(solution)/shard_map/ppermute | solution.py:314
  211.4 6.2 %collective-permute-start.26 = (bf16[512,1024]{1,0:T(8,128)(2,1)}, bf16[512,1024]{1,0:T(8,128)(2,1)}, u32[]{:S(2)}, u32[]{:S(2)}) collective-permute-start(bf16[512,1024]{1,0:T(8,128)(2,1)} %collective-permute-done.20.refs_8_), channel_id=1, source_target_pairs={{0,1},{1,0},{2,3},{3,2},{4,5},{5,4},{6,7},{7,6},{8,9},{9,8},{10,11... | collective-permute-start | bytes 3145736 | tf_op jit(solution)/shard_map/ppermute | solution.py:314
  213.1 25.1 %collective-permute-start.21 = (bf16[512,1024]{1,0:T(8,128)(2,1)}, bf16[512,1024]{1,0:T(8,128)(2,1)}, u32[]{:S(2)}, u32[]{:S(2)}) collective-permute-start(bf16[512,1024]{1,0:T(8,128)(2,1)} %collective-permute-done.20.refs_8_), channel_id=1, source_target_pairs={{0,16},{16,0},{1,17},{17,1},{2,18},{18,2},{3,19},{19,3},{4,20},{20... | collective-permute-start | bytes 3145736 | tf_op jit(solution)/shard_map/ppermute | solution.py:353
  213.8 3.1 %collective-permute-start.27 = (bf16[256,1024]{1,0:T(8,128)(2,1)}, bf16[256,1024]{1,0:T(8,128)(2,1)}, u32[]{:S(2)}, u32[]{:S(2)}) collective-permute-start(bf16[256,1024]{1,0:T(8,128)(2,1)} %collective-permute-done.12.refs_10_), channel_id=1, source_target_pairs={{0,1},{1,0},{2,3},{3,2},{4,5},{5,4},{6,7},{7,6},{8,9},{9,8},{10,11... | collective-permute-start | bytes 1572872 | tf_op jit(solution)/shard_map/ppermute | solution.py:314
  216.7 74.6 %collective-permute-start.28 = (bf16[3,64,5120]{2,1,0:T(8,128)(2,1)}, bf16[3,64,5120]{2,1,0:T(8,128)(2,1)}, u32[]{:S(2)}, u32[]{:S(2)}) collective-permute-start(bf16[3,64,5120]{2,1,0:T(8,128)(2,1)} %get-tuple-element.25.refs_0_), channel_id=1, source_target_pairs={{0,1},{1,0},{2,3},{3,2},{4,5},{5,4},{6,7},{7,6},{8,9},{9,8},{10,11... | collective-permute-start | bytes 5898248 | tf_op jit(solution)/shard_map/ppermute | solution.py:314
  216.9 45.5 %collective-permute-start.13 = (bf16[256,1024]{1,0:T(8,128)(2,1)}, bf16[256,1024]{1,0:T(8,128)(2,1)S(1)}, u32[]{:S(2)}, u32[]{:S(2)}) collective-permute-start(bf16[256,1024]{1,0:T(8,128)(2,1)} %collective-permute-done.12.refs_10_), channel_id=1, source_target_pairs={{0,16},{16,0},{1,17},{17,1},{2,18},{18,2},{3,19},{19,3},{4,20},{20... | collective-permute-start | bytes 1572872 | tf_op jit(solution)/shard_map/ppermute | solution.py:353
  217.7 45.3 %collective-permute-start.19 = (bf16[512,1024]{1,0:T(8,128)(2,1)}, bf16[512,1024]{1,0:T(8,128)(2,1)}, u32[]{:S(2)}, u32[]{:S(2)}) collective-permute-start(bf16[512,1024]{1,0:T(8,128)(2,1)} %collective-permute-done.18.refs_6_), channel_id=1, source_target_pairs={{0,1},{1,0},{2,3},{3,2},{4,5},{5,4},{6,7},{7,6},{8,9},{9,8},{10,11... | collective-permute-start | bytes 3145736 | tf_op jit(solution)/shard_map/ppermute | solution.py:314
  238.2 24.8 %collective-permute-start.22 = (bf16[512,1024]{1,0:T(8,128)(2,1)}, bf16[512,1024]{1,0:T(8,128)(2,1)}, u32[]{:S(2)}, u32[]{:S(2)}) collective-permute-start(bf16[512,1024]{1,0:T(8,128)(2,1)} %collective-permute-done.21.refs_8_), channel_id=1, source_target_pairs={{0,1},{1,0},{2,3},{3,2},{4,5},{5,4},{6,7},{7,6},{8,9},{9,8},{10,11... | collective-permute-start | bytes 3145736 | tf_op jit(solution)/shard_map/ppermute | solution.py:314
  239.4 23.1 %copy-start.2 = (bf16[3,64,5120]{2,1,0:T(8,128)(2,1)}, bf16[3,64,5120]{2,1,0:T(8,128)(2,1)S(1)}, u32[]{:S(2)}) copy-start(bf16[3,64,5120]{2,1,0:T(8,128)(2,1)S(1)} %collective-permute-done.29.refs_2_) | copy-start | bytes 5898244
  239.4 51.9 %collective-permute-start.30 = (bf16[3,64,5120]{2,1,0:T(8,128)(2,1)S(1)}, bf16[3,64,5120]{2,1,0:T(8,128)(2,1)}, u32[]{:S(2)}, u32[]{:S(2)}) collective-permute-start(bf16[3,64,5120]{2,1,0:T(8,128)(2,1)S(1)} %collective-permute-done.29.refs_2_), channel_id=1, source_target_pairs={{0,1},{1,0},{2,3},{3,2},{4,5},{5,4},{6,7},{7,6},{8,9},{9,8},{10,11... | collective-permute-start | bytes 5898248 | tf_op jit(solution)/shard_map/ppermute | solution.py:314
  262.5 21.3 %copy-start.7 = (bf16[256,1024]{1,0:T(8,128)(2,1)}, bf16[256,1024]{1,0:T(8,128)(2,1)S(1)}, u32[]{:S(2)}) copy-start(bf16[256,1024]{1,0:T(8,128)(2,1)S(1)} %collective-permute-done.13.refs_2_) | copy-start | bytes 1572868
  262.5 21.3 %collective-permute-start.14 = (bf16[256,1024]{1,0:T(8,128)(2,1)S(1)}, bf16[256,1024]{1,0:T(8,128)(2,1)S(1)}, u32[]{:S(2)}, u32[]{:S(2)}) collective-permute-start(bf16[256,1024]{1,0:T(8,128)(2,1)S(1)} %collective-permute-done.13.refs_2_), channel_id=1, source_target_pairs={{0,1},{1,0},{2,3},{3,2},{4,5},{5,4},{6,7},{7,6},{8,9},{9,8},{10,11... | collective-permute-start | bytes 1572872 | tf_op jit(solution)/shard_map/ppermute | solution.py:314
  283.8 0.8 copy-start.8
Sparse Core Ops, SparseCore 0:
  9.6 122.1 all-gather.1

commit v3 on v1

--- a/solution.py
+++ b/solution.py
@@ -9,8 +9,14 @@
 
 adapter_scale = 2.0
 factor_gradient = 0.0625
-vmem_bytes = 50 * 1024 * 1024
+vmem_bytes = 60 * 1024 * 1024
 bf16, f32, i32 = jnp.bfloat16, jnp.float32, jnp.int32
+
+
+def behind(value, *after):
+    if not after:
+        return value
+    return lax.optimization_barrier((value, *after))[0]
 
 
 def params(cost):
@@ -163,68 +169,133 @@
     )(live, here, there, hidden, grad)
 
 
-def base_kernel(pieces, count, scalars_ref, kept_ref, *refs):
-    w_refs = refs[:pieces]
-    coef_ref, block_ref = refs[pieces : pieces + 2]
-    out_ref = refs[-1]
-    deep = w_refs[0].shape[1]
+def base_kernel(n_dp, tiles, count, scalars_ref, kept_ref, *refs):
+    near = n_dp // 2
+    near_refs = refs[:near]
+    far_refs = refs[near : near + sum(tiles) * near]
+    coef_ref, block_ref = refs[near + sum(tiles) * near : near + sum(tiles) * near + 2]
+    out_ref, kept, weight, factor, result, kept_sem, in_sem, factor_sem, out_sem = refs[-9:]
+    _, tile, depth = weight.shape
+    deep = depth // n_dp
     height = coef_ref.shape[1]
-    total = None
-    for r in range(pieces):
-        start = pl.multiple_of(scalars_ref[1 + r] * deep, deep)
-        part = lax.dot_general(
-            kept_ref[:, pl.ds(start, deep)],
-            w_refs[r][...],
-            (((1,), (1,)), ((), ())),
-            preferred_element_type=f32,
+    steps = len(tiles)
+
+    def lanes(r):
+        return pl.ds(pl.multiple_of(scalars_ref[steps + r] * deep, deep), deep)
+
+    def span(j):
+        return pl.ds(pl.multiple_of(scalars_ref[j] * tile, tile), tile)
+
+    def loads(j, slot):
+        copies = [
+            pltpu.make_async_copy(
+                near_refs[r].at[span(j), :], weight.at[slot, :, lanes(r)], in_sem.at[slot, r]
+            )
+            for r in range(near)
+        ]
+        first = sum(tiles[:j]) * near
+        part = tile // tiles[j]
+        for k in range(tiles[j]):
+            for r in range(near):
+                copies.append(
+                    pltpu.make_async_copy(
+                        far_refs[first + k * near + r],
+                        weight.at[slot, pl.ds(k * part, part), lanes(near + r)],
+                        in_sem.at[slot, (k + 1) * near + r],
+                    )
+                )
+        copies.append(
+            pltpu.make_async_copy(
+                block_ref.at[:, :, span(j)], factor.at[slot], factor_sem.at[slot]
+            )
         )
-        total = part if total is None else total + part
-    for b in range(count):
-        extra = jnp.dot(coef_ref[b], block_ref[b], preferred_element_type=f32)
-        here = total[b * height : (b + 1) * height] + extra
-        valid = lax.broadcasted_iota(i32, here.shape, 0) < scalars_ref[1 + pieces + b]
-        out_ref[b * height : (b + 1) * height, :] = jnp.where(valid, here, 0.0).astype(bf16)
-
-
-def base(scalars, kept, whole, chunk, coef, block_a, held, size, tile):
+        return copies
+
+    def store(j, slot):
+        return pltpu.make_async_copy(
+            result.at[slot], out_ref.at[:, span(j)], out_sem.at[slot]
+        )
+
+    whole = pltpu.make_async_copy(kept_ref, kept, kept_sem)
+    whole.start()
+    for copy in loads(0, 0):
+        copy.start()
+    whole.wait()
+
+    @pl.loop(0, steps)
+    def _(step):
+        slot = lax.rem(step, 2)
+        for j in range(steps):
+
+            @pl.when(step == j)
+            def _():
+                if j + 1 < steps:
+                    for copy in loads(j + 1, (j + 1) % 2):
+                        copy.start()
+                for copy in loads(j, j % 2):
+                    copy.wait()
+                if j >= 2:
+                    store(j - 2, j % 2).wait()
+
+        total = lax.dot_general(
+            kept[...], weight[slot], (((1,), (1,)), ((), ())), preferred_element_type=f32
+        )
+        for b in range(count):
+            extra = jnp.dot(coef_ref[b], factor[slot, b], preferred_element_type=f32)
+            here = total[b * height : (b + 1) * height] + extra
+            valid = lax.broadcasted_iota(i32, here.shape, 0) < scalars_ref[steps + n_dp + b]
+            result[slot, b * height : (b + 1) * height, :] = jnp.where(valid, here, 0.0).astype(
+                bf16
+            )
+        for j in range(steps):
+            pl.when(step == j)(lambda j=j: store(j, j % 2).start())
+
+    for j in range(max(steps - 2, 0), steps):
+        store(j, j % 2).wait()
+
+
+def base(places, scalars, kept, near, tiles, coef, block_a, held):
     rows, depth = kept.shape
     count, rank, ff = block_a.shape
-    pieces = len(whole) + len(chunk)
-    deep = depth // pieces
-    height = rows // count
-    once2 = lambda i, s: (0, 0)
-    placed = lambda i, s: (s[0] + i, 0)
-    in_specs = [pl.BlockSpec((rows, depth), once2)]
-    operands = [kept]
-    for r in range(pieces):
-        if r in whole:
-            in_specs.append(pl.BlockSpec((tile, deep), placed))
-            operands.append(whole[r])
-        else:
-            in_specs.append(pl.BlockSpec((tile, deep), lambda i, s: (i, 0)))
-            operands.append(chunk[r])
-    in_specs += [
-        pl.BlockSpec((count, height, rank), lambda i, s: (0, 0, 0)),
-        pl.BlockSpec((count, rank, tile), lambda i, s: (0, 0, s[0] + i)),
-    ]
+    top = len(near)
+    tile = sum(piece[top].shape[0] for piece in tiles[0])
+    anywhere = pl.BlockSpec(memory_space=pl.ANY)
+    operands = [kept] + [near[r] for r in range(top)]
+    for pieces in tiles:
+        for piece in pieces:
+            operands += [piece[r] for r in range(top, 2 * top)]
+    in_specs = [anywhere] * len(operands)
+    in_specs += [pl.BlockSpec(coef.shape, lambda i, s: (0, 0, 0)), anywhere]
     operands += [coef, block_a]
     aliases = {}
     if held is not None:
-        in_specs.append(pl.BlockSpec(memory_space=pl.ANY))
+        in_specs.append(anywhere)
         operands.append(held)
         aliases = {len(operands): 0}
+    most = max(len(pieces) for pieces in tiles)
+    span = tile * len(tiles)
     return pl.pallas_call(
-        functools.partial(base_kernel, pieces, count),
+        functools.partial(base_kernel, 2 * top, [len(pieces) for pieces in tiles], count),
         grid_spec=pltpu.PrefetchScalarGridSpec(
             num_scalar_prefetch=1,
-            grid=(size // tile,),
+            grid=(1,),
             in_specs=in_specs,
-            out_specs=pl.BlockSpec((rows, tile), lambda i, s: (0, s[0] + i)),
+            out_specs=anywhere,
+            scratch_shapes=[
+                pltpu.VMEM((rows, depth), bf16),
+                pltpu.VMEM((2, tile, depth), bf16),
+                pltpu.VMEM((2, count, rank, tile), bf16),
+                pltpu.VMEM((2, rows, tile), bf16),
+                pltpu.SemaphoreType.DMA,
+                pltpu.SemaphoreType.DMA((2, (1 + most) * top)),
+                pltpu.SemaphoreType.DMA((2,)),
+                pltpu.SemaphoreType.DMA((2,)),
+            ],
         ),
         out_shape=jax.ShapeDtypeStruct((rows, ff), bf16),
         input_output_aliases=aliases,
-        **params((2 * rows * depth * size, 2 * (rows * depth + (rows + depth) * size))),
-    )(scalars, *operands)
+        **params((2 * rows * depth * span, 2 * (rows * depth + (rows + depth) * span))),
+    )(jnp.concatenate([jnp.stack(places).astype(i32), scalars]), *operands)
 
 
 def merge_kernel(pieces, count, tiles, slots_ref, *refs):
@@ -266,6 +337,67 @@
         ],
         **params((0, both * rank * (2 * len(pieces) * count + 4 * local))),
     )(slots, *pieces)
+
+
+def add_kernel(pieces, count, slots_ref, *refs):
+    term_refs = refs[:pieces]
+    a_ref, b_ref, term, a, b, term_sem, a_sem, b_sem = refs[pieces + 2 :]
+    ff = a.shape[1]
+    for r in range(pieces):
+        for k in range(count):
+            slot = slots_ref[r * count + k]
+
+            @pl.when((slot >= 0) & (slot < a_ref.shape[0]))
+            def _():
+                loads = [
+                    pltpu.make_async_copy(term_refs[r].at[k], term, term_sem),
+                    pltpu.make_async_copy(a_ref.at[slot], a, a_sem),
+                    pltpu.make_async_copy(b_ref.at[slot], b, b_sem),
+                ]
+                for copy in loads:
+                    copy.start()
+                for copy in loads:
+                    copy.wait()
+                a[...] += term[:, :ff].astype(f32)
+                b[...] += term[:, ff:].astype(f32)
+                stores = [
+                    pltpu.make_async_copy(a, a_ref.at[slot], a_sem),
+                    pltpu.make_async_copy(b, b_ref.at[slot], b_sem),
+                ]
+                for copy in stores:
+                    copy.start()
+                for copy in stores:
+                    copy.wait()
+
+
+def add_far(slots, pieces, grad_a, grad_b):
+    count, rank, both = pieces[0].shape
+    ff, d = grad_a.shape[2], grad_b.shape[2]
+    anywhere = pl.BlockSpec(memory_space=pl.ANY)
+    n = len(pieces)
+    return pl.pallas_call(
+        functools.partial(add_kernel, n, count),
+        grid_spec=pltpu.PrefetchScalarGridSpec(
+            num_scalar_prefetch=1,
+            grid=(1,),
+            in_specs=[anywhere] * (n + 2),
+            out_specs=[anywhere] * 2,
+            scratch_shapes=[
+                pltpu.VMEM((rank, both), bf16),
+                pltpu.VMEM((rank, ff), f32),
+                pltpu.VMEM((rank, d), f32),
+                pltpu.SemaphoreType.DMA,
+                pltpu.SemaphoreType.DMA,
+                pltpu.SemaphoreType.DMA,
+            ],
+        ),
+        out_shape=[
+            jax.ShapeDtypeStruct(grad_a.shape, f32),
+            jax.ShapeDtypeStruct(grad_b.shape, f32),
+        ],
+        input_output_aliases={n + 1: 0, n + 2: 1},
+        **params((0, n * count * 10 * rank * both)),
+    )(slots, *pieces, grad_a, grad_b)
 
 
 def on_device(
@@ -308,72 +440,109 @@
 
     kept = lax.all_gather(output_gradient, "fsdp", axis=1, tiled=True)
 
+    share = ff // n_groups
+    if share % 1024 == 0:
+        tile = 512
+        rest = [(k * tile, tile) for k in range(1, share // tile)]
+        parts = [(0, tile // 2), *rest, (tile // 2, tile // 2)]
+        groups = [[k] for k in range(1, share // tile)] + [[0, share // tile]]
+    else:
+        tile = share
+        parts = [(0, share)]
+        groups = [[0]]
+    crossed = [None] * len(parts)
+    turned = [[] for _ in parts]
+    done = []
+
+    def flat(*pieces):
+        return [v for piece in pieces for v in piece.values()]
+
+    def sends(j, *after):
+        after = [*after, *done]
+        done.clear()
+        if j < len(parts):
+            start, size = parts[j]
+            piece = lax.dynamic_slice_in_dim(
+                frozen_down_weight, group * share + start, size, axis=0
+            )
+            crossed[j] = {top: swap(behind(piece, *after), top)}
+            done.extend(flat(crossed[j]))
+        if 0 <= j - 1 < len(parts):
+            piece = behind(crossed[j - 1][top], *after)
+            for shift in range(1, n_groups):
+                ring = [(i, (i + shift) % n_groups) for i in range(n_groups)]
+                turned[j - 1].append({top: lax.ppermute(piece, "groups", ring)})
+            crossed[j - 1] = spread({top: piece})
+            done.extend(flat(*turned[j - 1], crossed[j - 1]))
+        if 0 <= j - 2 < len(parts):
+            turned[j - 2] = [spread({top: behind(p[top], *after)}) for p in turned[j - 2]]
+            done.extend(flat(*turned[j - 2]))
+
+    sends(0, far_slots)
+
     first = jnp.swapaxes(adapter_first_factors, 1, 2)
     a_near = spread({0: first})
     b_near = spread({0: adapter_second_factors})
     near = sorted(a_near)
     a_near = [a_near[r] for r in near]
     b_near = [b_near[r] for r in near]
+    whole = spread({0: behind(frozen_down_weight, *a_near, *b_near)})
 
     def places(wanted):
         owner = wanted // local
         index = jnp.concatenate([wanted % local] * len(near))
         return index, jnp.where((owner ^ me) < top, owner ^ me, len(near))
 
-    far = swap(pick(*places(far_slots), a_near, b_near), top)
-
-    share = ff // n_groups
-    size = max(min(share, 256), share // 4)
-    tile = min(512, size)
-    shares = []
-    for j in range(share // size):
-        shares.append(
-            swap(
-                lax.dynamic_slice_in_dim(
-                    frozen_down_weight, group * share + j * size, size, axis=0
-                ),
-                top,
-            )
-        )
-    whole = spread({0: frozen_down_weight})
-
-    part, block_a = project(*places(slots), a_near, b_near, far, hidden, output_gradient)
+    far = swap(pick(*places(behind(far_slots, *done)), a_near, b_near), top)
+    both_slots = spread({0: jnp.concatenate([slots, far_slots])})
+    sends(1, far)
+
+    ready = behind(slots, *whole.values(), *both_slots.values())
+    part, block_a = project(*places(ready), a_near, b_near, far, hidden, output_gradient)
+    sends(2, part)
     bit = 1
     total = None
     while bit < n_fsdp:
         total = part if total is None else total + other
         other = swap(total, bit, "fsdp", n_fsdp)
         bit *= 2
+    sends(3, total)
     terms, coef = block_terms(island_live_rows, total, other, hidden, output_gradient)
-    far_terms = swap(terms, top)
-
-    order = [me ^ r for r in range(n_dp)]
+    far_terms = swap(behind(terms, *done), top)
+    for j in range(4, len(parts) + 2):
+        sends(j)
+    near_terms = spread({0: terms})
+
+    relative = [both_slots[r][:count] for r in near] + [both_slots[r][count:] for r in near]
+    relative = jnp.concatenate(relative) - me * local
+    edge = count * len(near)
+    grad_a, grad_b = merge(relative[:edge], [near_terms[r] for r in near], local, ff, d)
+
+    scalars = jnp.concatenate([jnp.stack([me ^ r for r in range(n_dp)]).astype(i32), island_live_rows])
+    arrived = []
+    for shift in range(n_groups):
+        pieces = [turned[j][shift - 1] if shift else crossed[j] for j in range(len(parts))]
+        start = lax.rem(group + n_groups - shift, n_groups) * share
+        arrived.append(
+            [((start + parts[g[0]][0]) // tile, [pieces[j] for j in g]) for g in groups]
+        )
+    if len(groups) > 1:
+        calls = [tiles[:-1] for tiles in arrived] + [[tiles[-1] for tiles in arrived]]
+    else:
+        calls = arrived
     grad_hidden = None
-    for shift in range(n_groups):
-        for j, piece in enumerate(shares):
-            if shift:
-                piece = lax.ppermute(
-                    piece, "groups", [(i, (i + shift) % n_groups) for i in range(n_groups)]
-                )
-            start = lax.rem(group + n_groups - shift, n_groups) * share + j * size
-            scalars = jnp.stack([start // tile] + order).astype(i32)
-            grad_hidden = base(
-                jnp.concatenate([scalars, island_live_rows]),
-                kept,
-                whole,
-                spread({top: piece}),
-                coef,
-                block_a,
-                grad_hidden,
-                size,
-                tile,
-            )
-
-    all_slots = spread({0: slots, top: far_slots})
-    all_terms = spread({0: terms, top: far_terms})
-    keys = sorted(all_terms)
-    relative = jnp.concatenate([all_slots[r] for r in keys]) - me * local
-    grad_a, grad_b = merge(relative, [all_terms[r] for r in keys], local, ff, min(d, 512))
+    stages = [grad_a]
+    for tiles in calls:
+        where = [place for place, _ in tiles]
+        pieces = [piece for _, piece in tiles]
+        grad_hidden = base(where, scalars, kept, whole, pieces, coef, block_a, grad_hidden)
+        stages.append(grad_hidden)
+
+    far_terms = behind(far_terms, *stages[:3:2], *flat(*sum(turned, [])))
+    all_far = spread({top: far_terms})
+    grad_a, grad_b = add_far(
+        relative[edge:], [all_far[r + top] for r in near], grad_a, grad_b
+    )
     return grad_hidden, jnp.swapaxes(grad_a, 1, 2), grad_b
 
 

time: 333 us -> 277 us (0.83)
  the two profiles are of different devices: /device:TPU:11 before, /device:TPU:14 now
where the time goes in v3:
time: 277 us; the launch traced here: 275 us
  waiting for transfers between devices  139 us (50%)
  Pallas kernels  87.9 us (32%)
  starting transfers between devices  19.1 us (7%)
  between operations  14.3 us (5%)
  local copies, waits for them, and re-layouts  10.7 us (4%)
  other arithmetic  4.3 us (2%)
    ppermute x26, waiting for transfers between devices, swap(): return lax.ppermute(value, axis, [(i, i ^ bit) for i in range(size)])  129 us
    pallas_call x3, Pallas kernels, base(): pl.pallas_call(functools.partial(base_kernel, 2 * top, [len(pieces) for p...  49.1 us
    ppermute x26, starting transfers between devices, swap(): return lax.ppermute(value, axis, [(i, i ^ bit) for i in range(size)])  14.4 us
    pallas_call x1, Pallas kernels, add_far(): pl.pallas_call(functools.partial(add_kernel, n, count), grid_spec=pltpu.P...  11.1 us
    ppermute x5, waiting for transfers between devices, sends(): turned[j - 1].append({top: lax.ppermute(piece, 'groups', ring)})  9.81 us
    pallas_call x1, Pallas kernels, project(): pl.pallas_call(functools.partial(project_kernel, pieces), grid_spec=pltpu...  8.06 us
    pallas_call x1, Pallas kernels, merge(): pl.pallas_call(functools.partial(merge_kernel, len(pieces), count, tiles)...  8 us
    pallas_call x1, Pallas kernels, block_terms(): pl.pallas_call(terms_kernel, grid_spec=pltpu.PrefetchScalarGridSpec(num_s...  7.01 us
  transfers between devices with their start and end apart: 32, of which 13 were waited for; matrix products, arithmetic and copies ran while one was open for 5% of the time, Pallas kernels for 28%

profile of v3, /device:TPU:14, one launch (start us, length us, event | category | flops | bytes accessed | tf_op | source)
XLA Modules:
  0.0 275.0 jit_solution(13783336414562814114)
XLA Ops:
  7.2 0.1 collective-permute-start
  7.3 0.5 collective-permute-start.1
  7.8 8.0 %collective-permute-done.1.refs_3_ = bf16[8,64,1024]{2,1,0:T(8,128)(2,1)S(1)} collective-permute-done((bf16[8,64,1024]{2,1,0:T(8,128)(2,1)}, bf16[8,64,1024]{2,1,0:T(8,128)(2,1)S(1)}, u32[]{:S(2)}, u32[]{:S(2)}) %collective-permute-start.1) | collective-permute-done | bytes 1048608 | tf_op jit(solution)/shard_map/ppermute | solution.py:426
  15.8 0.5 collective-permute-done.refs_1_
  16.3 0.1 collective-permute-start.2
  16.4 0.9 select_reduce_fusion
  17.3 0.6 collective-permute-start.3
  17.9 2.1 constant_dynamic-slice_fusion.3
  20.0 0.9 collective-permute-done.3
  20.9 0.6 collective-permute-start.4
  21.5 12.6 %collective-permute-done.4.refs_2_ = bf16[256,1024]{1,0:T(8,128)(2,1)} collective-permute-done((bf16[256,1024]{1,0:T(8,128)(2,1)S(1)}, bf16[256,1024]{1,0:T(8,128)(2,1)}, u32[]{:S(2)}, u32[]{:S(2)}) %collective-permute-start.4) | collective-permute-done | bytes 524320 | tf_op jit(solution)/shard_map/ppermute | solution.py:426
  34.0 0.5 compare_select_fusion.1
  34.6 0.6 pad_add_fusion.index_ref
  35.1 4.7 %shard_map.103 = bf16[3,64,5120]{2,1,0:T(8,128)(2,1)} custom-call(s32[6]{0:T(128)} %pad_add_fusion.index_ref, s32[3]{0:T(128)} %get-tuple-element.70.source_ref, bf16[8,64,4096]{2,1,0:T(8,128)(2,1)} %bitcast.15, bf16[8,64,4096]{2,1,0:T(8,128)(2,1)} %collective-permute-done.refs_1_, bf16[8,64,1024]{2,1,0:T(8,128)(2,1)} %refs_2_.3, bf16[8,64,1024]{2,1,0:T(8,128)(2,1)} %copy-done), custom_call_target="tpu_custom_call" | custom-call | bytes 5898240 | tf_op jit(solution)/shard_map/pallas_call | solution.py:54
  39.8 1.5 collective-permute-start.5
  41.3 3.5 %constant_dynamic-slice_fusion = (bf16[512,1024]{1,0:T(8,128)(2,1)}, bf16[512,1024]{1,0:T(8,128)(2,1)}, bf16[512,1024]{1,0:T(8,128)(2,1)S(1)}) fusion(bf16[4096,1024]{1,0:T(8,128)(2,1)} %refs_0_.2, s32[]{:T(128)S(6)} %select_n.83, s32[]{:T(128)S(6)} %select_n.78, s32[]{:T(128)S(6)} %select_n.82), kind=kLoop, calls=%fused_computation.7 | loop fusion | bytes 6291468 | tf_op jit(solution)/shard_map/dynamic_slice | solution.py:465
  44.8 38.9 %collective-permute-done.5.refs_4_ = bf16[3,64,5120]{2,1,0:T(8,128)(2,1)S(1)} collective-permute-done((bf16[3,64,5120]{2,1,0:T(8,128)(2,1)}, bf16[3,64,5120]{2,1,0:T(8,128)(2,1)S(1)}, u32[]{:S(2)}, u32[]{:S(2)}) %collective-permute-start.5) | collective-permute-done | bytes 1966112 | tf_op jit(solution)/shard_map/ppermute | solution.py:426
  83.8 1.7 collective-permute-start.9
  85.5 0.5 collective-permute-start.10
  86.0 0.1 pad_add_fusion.1
  86.1 0.5 collective-permute-start.7
  86.6 1.3 collective-permute-done.7
  87.9 0.5 compare_select_fusion
  88.4 0.6 pad_add_fusion.2.index_ref
  89.1 8.1 %shard_map.104 = (f32[3,256,128]{2,1,0:T(8,128)}, bf16[3,64,4096]{2,1,0:T(8,128)(2,1)}) custom-call(s32[6]{0:T(128)} %pad_add_fusion.2.index_ref, s32[3]{0:T(128)} %get-tuple-element.68.source_ref, bf16[8,64,4096]{2,1,0:T(8,128)(2,1)} %bitcast.16, bf16[8,64,4096]{2,1,0:T(8,128)(2,1)} %collective-permute-done.refs_1_, bf16[8,64,1024]{2,1,0:T(8,128)(2,1)} %refs_2_.3, ...), custom_call_target="tpu_custom_call" | custom-call | flops 503316480 | bytes 15728640 | tf_op jit(solution)/shard_map/pallas_call | solution.py:95
  97.1 0.7 collective-permute-done.10.refs_6_
  97.8 9.7 %collective-permute-done.9.refs_2_ = bf16[512,1024]{1,0:T(8,128)(2,1)S(1)} collective-permute-done((bf16[512,1024]{1,0:T(8,128)(2,1)}, bf16[512,1024]{1,0:T(8,128)(2,1)S(1)}, u32[]{:S(2)}, u32[]{:S(2)}) %collective-permute-start.9) | collective-permute-done | bytes 1048608 | tf_op jit(solution)/shard_map/ppermute | solution.py:426
  107.5 1.7 collective-permute-start.11
  109.2 0.5 collective-permute-start.12
  109.7 0.2 collective-permute-start.14
  109.9 0.4 collective-permute-start.8
  110.4 26.6 %collective-permute-done.8 = f32[3,256,128]{2,1,0:T(8,128)S(1)} collective-permute-done((f32[3,256,128]{2,1,0:T(8,128)}, f32[3,256,128]{2,1,0:T(8,128)S(1)}, u32[]{:S(2)}, u32[]{:S(2)}) %collective-permute-start.8) | collective-permute-done | bytes 393248 | tf_op jit(solution)/shard_map/ppermute | solution.py:426
  137.0 1.0 add.91.here_ref
  138.0 3.4 %collective-permute-start.27 = (f32[3,256,128]{2,1,0:T(8,128)S(1)}, f32[3,256,128]{2,1,0:T(8,128)}, u32[]{:S(2)}, u32[]{:S(2)}) collective-permute-start(f32[3,256,128]{2,1,0:T(8,128)S(1)} %add.91.here_ref), channel_id=1, source_target_pairs={{0,8},{4,12},{8,0},{12,4},{1,9},{5,13},{9,1},{13,5},{2,10},{6,14},... | collective-permute-start | bytes 1179656 | tf_op jit(solution)/shard_map/ppermute | solution.py:426
  141.5 0.1 collective-permute-start.17
  141.5 0.6 collective-permute-start.16
  142.2 0.6 collective-permute-start.15
  142.7 14.7 %collective-permute-done.27.there_ref = f32[3,256,128]{2,1,0:T(8,128)} collective-permute-done((f32[3,256,128]{2,1,0:T(8,128)S(1)}, f32[3,256,128]{2,1,0:T(8,128)}, u32[]{:S(2)}, u32[]{:S(2)}) %collective-permute-start.27) | collective-permute-done | bytes 393248 | tf_op jit(solution)/shard_map/ppermute | solution.py:426
  157.5 7.0 %shard_map.105 = (bf16[3,64,5120]{2,1,0:T(8,128)(2,1)}, bf16[3,256,64]{2,1,0:T(8,128)(2,1)}) custom-call(s32[3]{0:T(128)} %live_ref.1, f32[3,256,128]{2,1,0:T(8,128)} %copy-done.4, f32[3,256,128]{2,1,0:T(8,128)} %collective-permute-done.27.there_ref, bf16[768,4096]{1,0:T(8,128)(2,1)} %hid_ref.1, bf16[768,1024]{1,0:T(8,128)(2,1)} %grad_ref.1), custom_call_target="tpu_custom_call" | custom-call | flops 503316480 | bytes 9830400 | tf_op jit(solution)/shard_map/pallas_call | solution.py:148
  164.5 0.1 collective-permute-start.29
  164.6 3.1 %collective-permute-done.15.refs_6_ = bf16[512,1024]{1,0:T(8,128)(2,1)} collective-permute-done((bf16[512,1024]{1,0:T(8,128)(2,1)}, bf16[512,1024]{1,0:T(8,128)(2,1)}, u32[]{:S(2)}, u32[]{:S(2)}) %collective-permute-start.15) | collective-permute-done | bytes 1048608 | tf_op jit(solution)/shard_map/ppermute | solution.py:426
  167.7 0.1 collective-permute-start.21
  167.8 1.5 collective-permute-start.20
  169.3 0.2 collective-permute-start.22
  169.5 0.6 collective-permute-start.19
  170.1 0.6 concatenate.30.scalars_ref
  170.7 0.6 concatenate.29.scalars_ref
  171.3 0.1 add_subtract_fusion
  171.4 12.5 %collective-permute-done.19.refs_4_ = bf16[256,1024]{1,0:T(8,128)(2,1)S(1)} collective-permute-done((bf16[256,1024]{1,0:T(8,128)(2,1)}, bf16[256,1024]{1,0:T(8,128)(2,1)S(1)}, u32[]{:S(2)}, u32[]{:S(2)}) %collective-permute-start.19) | collective-permute-done | bytes 524320 | tf_op jit(solution)/shard_map/ppermute | solution.py:426
  183.9 0.6 collective-permute-start.28
  184.4 9.1 %collective-permute-done.20.refs_6_ = bf16[512,1024]{1,0:T(8,128)(2,1)S(1)} collective-permute-done((bf16[512,1024]{1,0:T(8,128)(2,1)}, bf16[512,1024]{1,0:T(8,128)(2,1)S(1)}, u32[]{:S(2)}, u32[]{:S(2)}) %collective-permute-start.20) | collective-permute-done | bytes 1048608 | tf_op jit(solution)/shard_map/ppermute | solution.py:474
  193.6 0.6 fusion
  194.2 1.3 copy-done.1
  195.5 8.0 %shard_map.109 = (f32[8,64,4096]{2,1,0:T(8,128)}, f32[8,64,1024]{2,1,0:T(8,128)}) custom-call(s32[6]{0:T(128)} %get-tuple-element.64.slots_ref, bf16[3,64,5120]{2,1,0:T(8,128)(2,1)} %get-tuple-element.53.refs_0_, bf16[3,64,5120]{2,1,0:T(8,128)(2,1)} %copy-done.1), custom_call_target="tpu_custom_call" | custom-call | bytes 14417920 | tf_op jit(solution)/shard_map/pallas_call | solution.py:323
  203.5 1.4 collective-permute-start.24
  204.9 0.3 collective-permute-start.23
  205.3 17.6 %shard_map.106.refs_10_ = bf16[768,4096]{1,0:T(8,128)(2,1)} custom-call(s32[10]{0:T(128)} %concatenate.30.scalars_ref, bf16[768,4096]{1,0:T(8,128)(2,1)} %all-gather.2.cloned.1.call-done.kept_ref, bf16[4096,1024]{1,0:T(8,128)(2,1)} %refs_0_.2, bf16[4096,1024]{1,0:T(8,128)(2,1)} %collective-permute-done.2.refs_1_, bf16[512,1024]{1,0:T(8,128)(2,1)} %copy-done.5, ...), custom_call_target="tpu_custom_call" | custom-call | flops 9663676416 | bytes 21233664 | tf_op jit(solution)/shard_map/pallas_call | solution.py:277
  223.0 0.2 collective-permute-start.26
  223.2 17.5 %shard_map.107.refs_12_ = bf16[768,4096]{1,0:T(8,128)(2,1)} custom-call(s32[10]{0:T(128)} %concatenate.29.scalars_ref, bf16[768,4096]{1,0:T(8,128)(2,1)} %all-gather.2.cloned.1.call-done.kept_ref, bf16[4096,1024]{1,0:T(8,128)(2,1)} %refs_0_.2, bf16[4096,1024]{1,0:T(8,128)(2,1)} %collective-permute-done.2.refs_1_, ...), custom_call_target="tpu_custom_call", output_to_operand_aliasing={{}: (12, {})} | custom-call | flops 9663676416 | bytes 21233664 | tf_op jit(solution)/shard_map/pallas_call | solution.py:277
  240.8 0.4 collective-permute-start.30
  241.2 0.6 concatenate.25.scalars_ref
  241.9 13.9 %shard_map.108 = bf16[768,4096]{1,0:T(8,128)(2,1)} custom-call(s32[9]{0:T(128)} %concatenate.25.scalars_ref, bf16[768,4096]{1,0:T(8,128)(2,1)} %all-gather.2.cloned.1.call-done.kept_ref, bf16[4096,1024]{1,0:T(8,128)(2,1)} %refs_0_.2, bf16[4096,1024]{1,0:T(8,128)(2,1)} %collective-permute-done.2.refs_1_, ...), custom_call_target="tpu_custom_call", output_to_operand_aliasing={{}: (14, {})} | custom-call | flops 6442450944 | bytes 16252928 | tf_op jit(solution)/shard_map/pallas_call | solution.py:277
  255.8 1.3 copy-done.2
  257.1 11.1 %shard_map.110 = (f32[8,64,4096]{2,1,0:T(8,128)}, f32[8,64,1024]{2,1,0:T(8,128)}) custom-call(s32[6]{0:T(128)} %get-tuple-element.65.slots_ref, bf16[3,64,5120]{2,1,0:T(8,128)(2,1)} %collective-permute-done.28.refs_0_, bf16[3,64,5120]{2,1,0:T(8,128)(2,1)} %copy-done.2, ...), custom_call_target="tpu_custom_call", output_to_operand_aliasing={{0}: (3, {}), {1}: (4, {})} | custom-call | bytes 19660800 | tf_op jit(solution)/shard_map/pallas_call | solution.py:378
  (52 shorter events, 0.2 us)
Async XLA Ops:
  7.2 198.1 %all-gather.2.cloned.1.call-start = ((), (), s32[]{:S(2)}) async-start(), calls=%async_computation | async-start | bytes 7864320 | tf_op jit(solution)/shard_map/all_gather | solution.py:441
  7.2 9.1 %collective-permute-start = (bf16[8,64,4096]{2,1,0:T(8,128)(2,1)}, bf16[8,64,4096]{2,1,0:T(8,128)(2,1)}, u32[]{:S(2)}, u32[]{:S(2)}) collective-permute-start(bf16[8,64,4096]{2,1,0:T(8,128)(2,1)} %bitcast.14), channel_id=1, source_target_pairs={{0,1},{1,0},{2,3},{3,2},{4,5},{5,4},{6,7},{7,6},{8,9},{9,8},{10,11... | collective-permute-start | bytes 12582920 | tf_op jit(solution)/shard_map/ppermute | solution.py:426
  7.3 8.5 %collective-permute-start.1 = (bf16[8,64,1024]{2,1,0:T(8,128)(2,1)}, bf16[8,64,1024]{2,1,0:T(8,128)(2,1)S(1)}, u32[]{:S(2)}, u32[]{:S(2)}) collective-permute-start(bf16[8,64,1024]{2,1,0:T(8,128)(2,1)} %refs_2_.3), channel_id=1, source_target_pairs={{0,1},{1,0},{2,3},{3,2},{4,5},{5,4},{6,7},{7,6},{8,9},{9,8},{10,11... | collective-permute-start | bytes 3145736 | tf_op jit(solution)/shard_map/ppermute | solution.py:426
  15.8 19.3 %copy-start = (bf16[8,64,1024]{2,1,0:T(8,128)(2,1)}, bf16[8,64,1024]{2,1,0:T(8,128)(2,1)S(1)}, u32[]{:S(2)}) copy-start(bf16[8,64,1024]{2,1,0:T(8,128)(2,1)S(1)} %collective-permute-done.1.refs_3_) | copy-start | bytes 3145732
  16.3 71.6 %collective-permute-start.2 = (bf16[4096,1024]{1,0:T(8,128)(2,1)}, bf16[4096,1024]{1,0:T(8,128)(2,1)}, u32[]{:S(2)}, u32[]{:S(2)}) collective-permute-start(bf16[4096,1024]{1,0:T(8,128)(2,1)} %refs_0_.2), channel_id=1, source_target_pairs={{0,1},{1,0},{2,3},{3,2},{4,5},{5,4},{6,7},{7,6},{8,9},{9,8},{10,11... | collective-permute-start | bytes 25165832 | tf_op jit(solution)/shard_map/ppermute | solution.py:426
  17.3 3.6 %collective-permute-start.3 = (s32[3]{0:T(128)S(1)}, s32[3]{0:T(128)S(1)}, u32[]{:S(2)}, u32[]{:S(2)}) collective-permute-start(s32[3]{0:T(128)S(1)} %select_reduce_fusion), channel_id=1, source_target_pairs={{0,2},{1,3},{2,0},{3,1},{4,6},{5,7},{6,4},{7,5},{8,10},{9,11},{10,... | collective-permute-start | bytes 44 | tf_op jit(solution)/shard_map/ppermute | solution.py:426
  20.9 13.1 %collective-permute-start.4 = (bf16[256,1024]{1,0:T(8,128)(2,1)S(1)}, bf16[256,1024]{1,0:T(8,128)(2,1)}, u32[]{:S(2)}, u32[]{:S(2)}) collective-permute-start(bf16[256,1024]{1,0:T(8,128)(2,1)S(1)} %get-tuple-element.32), channel_id=1, source_target_pairs={{0,2},{1,3},{2,0},{3,1},{4,6},{5,7},{6,4},{7,5},{8,10},{9,11},{10,... | collective-permute-start | bytes 1572872 | tf_op jit(solution)/shard_map/ppermute | solution.py:426
  39.8 43.9 %collective-permute-start.5 = (bf16[3,64,5120]{2,1,0:T(8,128)(2,1)}, bf16[3,64,5120]{2,1,0:T(8,128)(2,1)S(1)}, u32[]{:S(2)}, u32[]{:S(2)}) collective-permute-start(bf16[3,64,5120]{2,1,0:T(8,128)(2,1)} %shard_map.103), channel_id=1, source_target_pairs={{0,2},{1,3},{2,0},{3,1},{4,6},{5,7},{6,4},{7,5},{8,10},{9,11},{10,... | collective-permute-start | bytes 5898248 | tf_op jit(solution)/shard_map/ppermute | solution.py:426
  83.8 5.3 %copy-start.3 = (bf16[3,64,5120]{2,1,0:T(8,128)(2,1)}, bf16[3,64,5120]{2,1,0:T(8,128)(2,1)S(1)}, u32[]{:S(2)}) copy-start(bf16[3,64,5120]{2,1,0:T(8,128)(2,1)S(1)} %collective-permute-done.5.refs_4_) | copy-start | bytes 5898244
  83.8 23.7 %collective-permute-start.9 = (bf16[512,1024]{1,0:T(8,128)(2,1)}, bf16[512,1024]{1,0:T(8,128)(2,1)S(1)}, u32[]{:S(2)}, u32[]{:S(2)}) collective-permute-start(bf16[512,1024]{1,0:T(8,128)(2,1)} %get-tuple-element.37), channel_id=1, source_target_pairs={{0,2},{1,3},{2,0},{3,1},{4,6},{5,7},{6,4},{7,5},{8,10},{9,11},{10,... | collective-permute-start | bytes 3145736 | tf_op jit(solution)/shard_map/ppermute | solution.py:426
  85.5 12.3 %collective-permute-start.10 = (bf16[256,1024]{1,0:T(8,128)(2,1)}, bf16[256,1024]{1,0:T(8,128)(2,1)}, u32[]{:S(2)}, u32[]{:S(2)}) collective-permute-start(bf16[256,1024]{1,0:T(8,128)(2,1)} %collective-permute-done.4.refs_2_), channel_id=1, source_target_pairs={{0,16},{16,0},{1,17},{17,1},{2,18},{18,2},{3,19},{19,3},{4,20},{20... | collective-permute-start | bytes 1572872 | tf_op jit(solution)/shard_map/ppermute | solution.py:474
  86.0 11.8 %collective-permute-start.6 = (bf16[256,1024]{1,0:T(8,128)(2,1)}, bf16[256,1024]{1,0:T(8,128)(2,1)}, u32[]{:S(2)}, u32[]{:S(2)}) collective-permute-start(bf16[256,1024]{1,0:T(8,128)(2,1)} %collective-permute-done.4.refs_2_), channel_id=1, source_target_pairs={{0,1},{1,0},{2,3},{3,2},{4,5},{5,4},{6,7},{7,6},{8,9},{9,8},{10,11... | collective-permute-start | bytes 1572872 | tf_op jit(solution)/shard_map/ppermute | solution.py:426
  86.1 1.8 collective-permute-start.7
  107.5 57.0 %copy-start.5 = (bf16[512,1024]{1,0:T(8,128)(2,1)}, bf16[512,1024]{1,0:T(8,128)(2,1)S(1)}, u32[]{:S(2)}) copy-start(bf16[512,1024]{1,0:T(8,128)(2,1)S(1)} %collective-permute-done.9.refs_2_) | copy-start | bytes 3145732
  107.5 34.0 %collective-permute-start.11 = (bf16[512,1024]{1,0:T(8,128)(2,1)S(1)}, bf16[512,1024]{1,0:T(8,128)(2,1)}, u32[]{:S(2)}, u32[]{:S(2)}) collective-permute-start(bf16[512,1024]{1,0:T(8,128)(2,1)S(1)} %get-tuple-element.38), channel_id=1, source_target_pairs={{0,2},{1,3},{2,0},{3,1},{4,6},{5,7},{6,4},{7,5},{8,10},{9,11},{10,... | collective-permute-start | bytes 3145736 | tf_op jit(solution)/shard_map/ppermute | solution.py:426
  109.2 32.2 %collective-permute-start.13 = (bf16[512,1024]{1,0:T(8,128)(2,1)S(1)}, bf16[512,1024]{1,0:T(8,128)(2,1)S(1)}, u32[]{:S(2)}, u32[]{:S(2)}) collective-permute-start(bf16[512,1024]{1,0:T(8,128)(2,1)S(1)} %collective-permute-done.9.refs_2_), channel_id=1, source_target_pairs={{0,1},{1,0},{2,3},{3,2},{4,5},{5,4},{6,7},{7,6},{8,9},{9,8},{10,11... | collective-permute-start | bytes 3145736 | tf_op jit(solution)/shard_map/ppermute | solution.py:426
  109.2 32.2 %collective-permute-start.12 = (bf16[512,1024]{1,0:T(8,128)(2,1)S(1)}, bf16[512,1024]{1,0:T(8,128)(2,1)}, u32[]{:S(2)}, u32[]{:S(2)}) collective-permute-start(bf16[512,1024]{1,0:T(8,128)(2,1)S(1)} %collective-permute-done.9.refs_2_), channel_id=1, source_target_pairs={{0,16},{16,0},{1,17},{17,1},{2,18},{18,2},{3,19},{19,3},{4,20},{20... | collective-permute-start | bytes 3145736 | tf_op jit(solution)/shard_map/ppermute | solution.py:474
  109.7 31.7 %collective-permute-start.14 = (bf16[256,1024]{1,0:T(8,128)(2,1)}, bf16[256,1024]{1,0:T(8,128)(2,1)S(1)}, u32[]{:S(2)}, u32[]{:S(2)}) collective-permute-start(bf16[256,1024]{1,0:T(8,128)(2,1)} %collective-permute-done.10.refs_6_), channel_id=1, source_target_pairs={{0,1},{1,0},{2,3},{3,2},{4,5},{5,4},{6,7},{7,6},{8,9},{9,8},{10,11... | collective-permute-start | bytes 1572872 | tf_op jit(solution)/shard_map/ppermute | solution.py:426
  109.9 27.0 %collective-permute-start.8 = (f32[3,256,128]{2,1,0:T(8,128)}, f32[3,256,128]{2,1,0:T(8,128)S(1)}, u32[]{:S(2)}, u32[]{:S(2)}) collective-permute-start(f32[3,256,128]{2,1,0:T(8,128)} %get-tuple-element.36), channel_id=1, source_target_pairs={{0,4},{4,0},{8,12},{12,8},{1,5},{5,1},{9,13},{13,9},{2,6},{6,2},{1... | collective-permute-start | bytes 1179656 | tf_op jit(solution)/shard_map/ppermute | solution.py:426
  138.0 19.4 %copy-start.4 = (f32[3,256,128]{2,1,0:T(8,128)}, f32[3,256,128]{2,1,0:T(8,128)S(1)}, u32[]{:S(2)}) copy-start(f32[3,256,128]{2,1,0:T(8,128)S(1)} %add.91.here_ref) | copy-start | bytes 1179652
  138.0 19.4 %collective-permute-start.27 = (f32[3,256,128]{2,1,0:T(8,128)S(1)}, f32[3,256,128]{2,1,0:T(8,128)}, u32[]{:S(2)}, u32[]{:S(2)}) collective-permute-start(f32[3,256,128]{2,1,0:T(8,128)S(1)} %add.91.here_ref), channel_id=1, source_target_pairs={{0,8},{4,12},{8,0},{12,4},{1,9},{5,13},{9,1},{13,5},{2,10},{6,14},... | collective-permute-start | bytes 1179656 | tf_op jit(solution)/shard_map/ppermute | solution.py:426
  141.4 23.1 %copy-start.8 = (bf16[256,1024]{1,0:T(8,128)(2,1)}, bf16[256,1024]{1,0:T(8,128)(2,1)S(1)}, u32[]{:S(2)}) copy-start(bf16[256,1024]{1,0:T(8,128)(2,1)S(1)} %collective-permute-done.14.refs_7_) | copy-start | bytes 1572868
  141.4 23.1 %copy-start.6 = (bf16[512,1024]{1,0:T(8,128)(2,1)}, bf16[512,1024]{1,0:T(8,128)(2,1)S(1)}, u32[]{:S(2)}) copy-start(bf16[512,1024]{1,0:T(8,128)(2,1)S(1)} %collective-permute-done.13.refs_3_) | copy-start | bytes 3145732
  141.5 26.2 %collective-permute-start.17 = (bf16[512,1024]{1,0:T(8,128)(2,1)}, bf16[512,1024]{1,0:T(8,128)(2,1)}, u32[]{:S(2)}, u32[]{:S(2)}) collective-permute-start(bf16[512,1024]{1,0:T(8,128)(2,1)} %collective-permute-done.11.refs_4_), channel_id=1, source_target_pairs={{0,1},{1,0},{2,3},{3,2},{4,5},{5,4},{6,7},{7,6},{8,9},{9,8},{10,11... | collective-permute-start | bytes 3145736 | tf_op jit(solution)/shard_map/ppermute | solution.py:426
  141.5 26.2 %collective-permute-start.16 = (bf16[512,1024]{1,0:T(8,128)(2,1)}, bf16[512,1024]{1,0:T(8,128)(2,1)}, u32[]{:S(2)}, u32[]{:S(2)}) collective-permute-start(bf16[512,1024]{1,0:T(8,128)(2,1)} %collective-permute-done.11.refs_4_), channel_id=1, source_target_pairs={{0,16},{16,0},{1,17},{17,1},{2,18},{18,2},{3,19},{19,3},{4,20},{20... | collective-permute-start | bytes 3145736 | tf_op jit(solution)/shard_map/ppermute | solution.py:474
  142.2 27.9 %copy-start.13 = (s32[3]{0:T(128)S(1)}, s32[3]{0:T(128)}, u32[]{:S(2)}) copy-start(s32[3]{0:T(128)} %live_ref.1) | copy-start | bytes 40
  142.2 25.5 %collective-permute-start.15 = (bf16[512,1024]{1,0:T(8,128)(2,1)}, bf16[512,1024]{1,0:T(8,128)(2,1)}, u32[]{:S(2)}, u32[]{:S(2)}) collective-permute-start(bf16[512,1024]{1,0:T(8,128)(2,1)} %get-tuple-element.41), channel_id=1, source_target_pairs={{0,2},{1,3},{2,0},{3,1},{4,6},{5,7},{6,4},{7,5},{8,10},{9,11},{10,... | collective-permute-start | bytes 3145736 | tf_op jit(solution)/shard_map/ppermute | solution.py:426
  142.7 25.0 %collective-permute-start.18 = (bf16[512,1024]{1,0:T(8,128)(2,1)}, bf16[512,1024]{1,0:T(8,128)(2,1)}, u32[]{:S(2)}, u32[]{:S(2)}) collective-permute-start(bf16[512,1024]{1,0:T(8,128)(2,1)} %collective-permute-done.12.refs_2_), channel_id=1, source_target_pairs={{0,1},{1,0},{2,3},{3,2},{4,5},{5,4},{6,7},{7,6},{8,9},{9,8},{10,11... | collective-permute-start | bytes 3145736 | tf_op jit(solution)/shard_map/ppermute | solution.py:426
  164.5 29.7 %collective-permute-start.29 = (bf16[3,64,5120]{2,1,0:T(8,128)(2,1)}, bf16[3,64,5120]{2,1,0:T(8,128)(2,1)S(1)}, u32[]{:S(2)}, u32[]{:S(2)}) collective-permute-start(bf16[3,64,5120]{2,1,0:T(8,128)(2,1)} %get-tuple-element.53.refs_0_), channel_id=1, source_target_pairs={{0,1},{1,0},{2,3},{3,2},{4,5},{5,4},{6,7},{7,6},{8,9},{9,8},{10,11... | collective-permute-start | bytes 5898248 | tf_op jit(solution)/shard_map/ppermute | solution.py:426
  167.7 16.7 %collective-permute-start.21 = (bf16[512,1024]{1,0:T(8,128)(2,1)}, bf16[512,1024]{1,0:T(8,128)(2,1)}, u32[]{:S(2)}, u32[]{:S(2)}) collective-permute-start(bf16[512,1024]{1,0:T(8,128)(2,1)} %collective-permute-done.15.refs_6_), channel_id=1, source_target_pairs={{0,1},{1,0},{2,3},{3,2},{4,5},{5,4},{6,7},{7,6},{8,9},{9,8},{10,11... | collective-permute-start | bytes 3145736 | tf_op jit(solution)/shard_map/ppermute | solution.py:426
  167.8 25.8 %collective-permute-start.20 = (bf16[512,1024]{1,0:T(8,128)(2,1)}, bf16[512,1024]{1,0:T(8,128)(2,1)S(1)}, u32[]{:S(2)}, u32[]{:S(2)}) collective-permute-start(bf16[512,1024]{1,0:T(8,128)(2,1)} %collective-permute-done.15.refs_6_), channel_id=1, source_target_pairs={{0,16},{16,0},{1,17},{17,1},{2,18},{18,2},{3,19},{19,3},{4,20},{20... | collective-permute-start | bytes 3145736 | tf_op jit(solution)/shard_map/ppermute | solution.py:474
  169.3 24.2 %collective-permute-start.22 = (bf16[512,1024]{1,0:T(8,128)(2,1)}, bf16[512,1024]{1,0:T(8,128)(2,1)}, u32[]{:S(2)}, u32[]{:S(2)}) collective-permute-start(bf16[512,1024]{1,0:T(8,128)(2,1)} %collective-permute-done.16.refs_4_), channel_id=1, source_target_pairs={{0,1},{1,0},{2,3},{3,2},{4,5},{5,4},{6,7},{7,6},{8,9},{9,8},{10,11... | collective-permute-start | bytes 3145736 | tf_op jit(solution)/shard_map/ppermute | solution.py:426
  169.5 14.4 %collective-permute-start.19 = (bf16[256,1024]{1,0:T(8,128)(2,1)}, bf16[256,1024]{1,0:T(8,128)(2,1)S(1)}, u32[]{:S(2)}, u32[]{:S(2)}) collective-permute-start(bf16[256,1024]{1,0:T(8,128)(2,1)} %get-tuple-element.44), channel_id=1, source_target_pairs={{0,2},{1,3},{2,0},{3,1},{4,6},{5,7},{6,4},{7,5},{8,10},{9,11},{10,... | collective-permute-start | bytes 1572872 | tf_op jit(solution)/shard_map/ppermute | solution.py:426
  183.9 39.0 %copy-start.9 = (bf16[256,1024]{1,0:T(8,128)(2,1)}, bf16[256,1024]{1,0:T(8,128)(2,1)S(1)}, u32[]{:S(2)}) copy-start(bf16[256,1024]{1,0:T(8,128)(2,1)S(1)} %collective-permute-done.19.refs_4_) | copy-start | bytes 1572868
  183.9 56.9 %collective-permute-start.28 = (bf16[3,64,5120]{2,1,0:T(8,128)(2,1)}, bf16[3,64,5120]{2,1,0:T(8,128)(2,1)}, u32[]{:S(2)}, u32[]{:S(2)}) collective-permute-start(bf16[3,64,5120]{2,1,0:T(8,128)(2,1)} %get-tuple-element.53.refs_0_), channel_id=1, source_target_pairs={{0,2},{1,3},{2,0},{3,1},{4,6},{5,7},{6,4},{7,5},{8,10},{9,11},{10,... | collective-permute-start | bytes 5898248 | tf_op jit(solution)/shard_map/ppermute | solution.py:426
  193.6 29.4 %copy-start.7 = (bf16[512,1024]{1,0:T(8,128)(2,1)}, bf16[512,1024]{1,0:T(8,128)(2,1)S(1)}, u32[]{:S(2)}) copy-start(bf16[512,1024]{1,0:T(8,128)(2,1)S(1)} %collective-permute-done.20.refs_6_) | copy-start | bytes 3145732
  193.6 29.4 %collective-permute-start.25 = (bf16[512,1024]{1,0:T(8,128)(2,1)S(1)}, bf16[512,1024]{1,0:T(8,128)(2,1)}, u32[]{:S(2)}, u32[]{:S(2)}) collective-permute-start(bf16[512,1024]{1,0:T(8,128)(2,1)S(1)} %collective-permute-done.20.refs_6_), channel_id=1, source_target_pairs={{0,1},{1,0},{2,3},{3,2},{4,5},{5,4},{6,7},{7,6},{8,9},{9,8},{10,11... | collective-permute-start | bytes 3145736 | tf_op jit(solution)/shard_map/ppermute | solution.py:426
  194.2 1.3 copy-start.1
  203.5 19.4 %collective-permute-start.24 = (bf16[256,1024]{1,0:T(8,128)(2,1)S(1)}, bf16[256,1024]{1,0:T(8,128)(2,1)S(1)}, u32[]{:S(2)}, u32[]{:S(2)}) collective-permute-start(bf16[256,1024]{1,0:T(8,128)(2,1)S(1)} %collective-permute-done.19.refs_4_), channel_id=1, source_target_pairs={{0,16},{16,0},{1,17},{17,1},{2,18},{18,2},{3,19},{19,3},{4,20},{20... | collective-permute-start | bytes 1572872 | tf_op jit(solution)/shard_map/ppermute | solution.py:474
  204.9 18.0 %collective-permute-start.23 = (bf16[256,1024]{1,0:T(8,128)(2,1)S(1)}, bf16[256,1024]{1,0:T(8,128)(2,1)S(1)}, u32[]{:S(2)}, u32[]{:S(2)}) collective-permute-start(bf16[256,1024]{1,0:T(8,128)(2,1)S(1)} %collective-permute-done.19.refs_4_), channel_id=1, source_target_pairs={{0,1},{1,0},{2,3},{3,2},{4,5},{5,4},{6,7},{7,6},{8,9},{9,8},{10,11... | collective-permute-start | bytes 1572872 | tf_op jit(solution)/shard_map/ppermute | solution.py:426
  223.0 17.8 %copy-start.10 = (bf16[256,1024]{1,0:T(8,128)(2,1)}, bf16[256,1024]{1,0:T(8,128)(2,1)S(1)}, u32[]{:S(2)}) copy-start(bf16[256,1024]{1,0:T(8,128)(2,1)S(1)} %collective-permute-done.24.refs_8_) | copy-start | bytes 1572868
  223.0 17.8 %copy-start.11 = (bf16[256,1024]{1,0:T(8,128)(2,1)}, bf16[256,1024]{1,0:T(8,128)(2,1)S(1)}, u32[]{:S(2)}) copy-start(bf16[256,1024]{1,0:T(8,128)(2,1)S(1)} %collective-permute-done.23.refs_5_) | copy-start | bytes 1572868
  223.0 17.8 %collective-permute-start.26 = (bf16[256,1024]{1,0:T(8,128)(2,1)S(1)}, bf16[256,1024]{1,0:T(8,128)(2,1)S(1)}, u32[]{:S(2)}, u32[]{:S(2)}) collective-permute-start(bf16[256,1024]{1,0:T(8,128)(2,1)S(1)} %collective-permute-done.24.refs_8_), channel_id=1, source_target_pairs={{0,1},{1,0},{2,3},{3,2},{4,5},{5,4},{6,7},{7,6},{8,9},{9,8},{10,11... | collective-permute-start | bytes 1572872 | tf_op jit(solution)/shard_map/ppermute | solution.py:426
  240.8 1.0 copy-start.12
  240.8 14.9 %collective-permute-start.30 = (bf16[3,64,5120]{2,1,0:T(8,128)(2,1)}, bf16[3,64,5120]{2,1,0:T(8,128)(2,1)S(1)}, u32[]{:S(2)}, u32[]{:S(2)}) collective-permute-start(bf16[3,64,5120]{2,1,0:T(8,128)(2,1)} %collective-permute-done.28.refs_0_), channel_id=1, source_target_pairs={{0,1},{1,0},{2,3},{3,2},{4,5},{5,4},{6,7},{7,6},{8,9},{9,8},{10,11... | collective-permute-start | bytes 5898248 | tf_op jit(solution)/shard_map/ppermute | solution.py:426
  255.8 1.3 copy-start.2
Sparse Core Ops, SparseCore 0:
  16.6 122.0 all-gather.1
